TPU v7x, 256 devices: a whole 4x4x8 slice. The times are simulated.
256 devices in a mesh: ctx: 32 (over x, z_hi, core), chan: 8 (over z_lo, y).
Axes of the slice: x: 4, y: 4, z: 8 (z_hi: 4, z_lo: 2; z = z_hi * 2 + z_lo), core: 2. Of those that a mesh axis runs over, the one named last changes fastest.
Arguments:
- loader_rows: bfloat16 [4096, 12288], P('ctx', 'chan'), parts along dimension 1, may hold values from -6 to 6
- row_pos: int32 [4096], P('ctx'), may hold values from 0 to 4095, as said below
- short_w: float32 [3, 12288], P(None, 'chan'), parts along dimension 1, may hold values from -3.5 to 3.5
- long_filter: float32 [4096, 4096], P('ctx', 'chan'), parts along dimension 1, may hold values from -4 to 4
- skip_gain: float32 [4096], P('chan'), parts along dimension 0, may hold values from -4 to 4
Outputs:
- gated_out: bfloat16 [4096, 4096], P('ctx', 'chan'), parts along dimension 1
There are 8 independent parts, one for each index of `chan`. A program takes and returns all parts, laid end to end along the dimension named above; an argument that names none is the same for every part. Nothing has to cross between parts.
Inputs may be any that keep to these rules, and one draw needn't show every extreme that they name: row_pos names every position once; position p belongs to index p // 128 of ctx; the 128 rows of one index of ctx hold at most 8 positions of any one index, and exactly 8 in every draw.
All inputs are finite; a program needn't handle non-finite values.
Results may differ from a plain program's by a relative error of at most 0.001.
Values may be sent and summed in bfloat16 or wider, within the bound.
A program may use at most 64 MiB of HBM per device.

v0:
```python
import math

import jax
import jax.numpy as jnp
from jax import lax
from jax.sharding import PartitionSpec as P

KS = 3


def passed_along(value, axis, steps):
    count = lax.axis_size(axis)
    initial, last = (max(0, -steps), min(count, count - steps))
    return lax.ppermute(value, axis, [(source, source + steps) for source in range(initial, last)])


def partner_2(value, axis, apart):
    mask = 2**apart
    pairs = [(source, source ^ mask) for source in range(lax.axis_size(axis))]
    return lax.ppermute(value, axis, pairs)


def rotate(real_part, imag_part, radians):
    cosine = jnp.cos(radians)
    sine = jnp.sin(radians)
    return (real_part * cosine - imag_part * sine, real_part * sine + imag_part * cosine)


def body(loader_rows, row_pos, short_w, long_filter, skip_gain):
    local_len = loader_rows.shape[0]
    channels = long_filter.shape[1]
    ctx_count = lax.axis_size("ctx")
    section_count = ctx_count.bit_length() - 1
    my_index = lax.axis_index("ctx")
    capacity = 2 * (local_len // ctx_count)
    spectrum_len = 2 * local_len * ctx_count
    owner_dev = row_pos // local_len
    within = row_pos % local_len
    onehot = (owner_dev[:, None] == jnp.arange(ctx_count, dtype=jnp.int32)[None, :]).astype(
        jnp.int32
    )
    slot_index = jnp.sum(jnp.cumsum(onehot, axis=0) * onehot, axis=1) - 1
    outgoing = (
        jnp.zeros((ctx_count, capacity, loader_rows.shape[1]), loader_rows.dtype)
        .at[owner_dev, slot_index]
        .set(loader_rows)
    )
    targets = (
        jnp.full((ctx_count, capacity), local_len, jnp.int32).at[owner_dev, slot_index].set(within)
    )
    arrived, places = (
        lax.all_to_all(outgoing, "ctx", split_axis=0, concat_axis=0, tiled=True),
        lax.all_to_all(targets, "ctx", split_axis=0, concat_axis=0, tiled=True),
    )
    flat_rows = arrived.reshape(ctx_count * capacity, arrived.shape[2])
    seq_rows = (
        jnp.zeros((local_len + 1, flat_rows.shape[1]), flat_rows.dtype)
        .at[places.reshape(-1)]
        .set(flat_rows)[:local_len]
    )
    last_rows = seq_rows[local_len - (KS - 1) :]
    before = passed_along(last_rows, "ctx", 1)
    padded = jnp.concatenate([before, seq_rows], axis=0)
    featured = jnp.zeros(seq_rows.shape, jnp.float32)
    for offset in range(KS):
        featured = featured + short_w[offset][None, :] * padded[
            KS - 1 - offset : KS - 1 - offset + local_len
        ].astype(jnp.float32)
    q_feat = featured[:, :channels]
    k_feat = featured[:, channels : 2 * channels]
    v_feat = featured[:, 2 * channels :]
    product = k_feat * v_feat
    source_real = jnp.stack([product, long_filter])
    source_imag = jnp.zeros_like(source_real)
    first_turn = -math.pi * my_index.astype(jnp.float32) / ctx_count
    odd_real, odd_imag = rotate(source_real, source_imag, first_turn)
    spectra = jnp.stack([jnp.stack([source_real, source_imag]), jnp.stack([odd_real, odd_imag])])
    for step_index in range(section_count):
        bit_pos = section_count - 1 - step_index
        half_span = 1 << bit_pos
        partner = partner_2(spectra, "ctx", bit_pos)
        on_upper = my_index >> bit_pos & 1 == 1
        turn_angle = -math.pi * (my_index & half_span - 1).astype(jnp.float32) / half_span
        lower_value = spectra + partner
        difference = partner - spectra
        diff_real, diff_imag = rotate(difference[:, 0], difference[:, 1], turn_angle)
        upper_value = jnp.stack([diff_real, diff_imag], axis=1)
        spectra = jnp.where(on_upper, upper_value, lower_value)
    spec_rank = jnp.zeros((), jnp.int32)
    for bit_pos in range(section_count):
        spec_rank = spec_rank + ((my_index >> bit_pos & 1) << section_count - 1 - bit_pos)
    positions = jnp.arange(local_len, dtype=jnp.int32)
    freq_pair = 2 * spec_rank + jnp.arange(2, dtype=jnp.int32)
    twiddle = (positions[None, :] * freq_pair[:, None] % spectrum_len).astype(jnp.float32) * (
        -2.0 * math.pi / spectrum_len
    )
    rot_real, rot_imag = rotate(spectra[:, 0], spectra[:, 1], twiddle[:, None, :, None])
    phase_grid = (positions[:, None] * positions[None, :] % local_len).astype(jnp.float32) * (
        2.0 * math.pi / local_len
    )
    cos_grid = jnp.cos(phase_grid)
    sin_grid = jnp.sin(phase_grid)
    spec_real = jnp.einsum(
        "kj,pwjc->pwkc", cos_grid, rot_real, precision=lax.Precision.HIGHEST
    ) + jnp.einsum("kj,pwjc->pwkc", sin_grid, rot_imag, precision=lax.Precision.HIGHEST)
    spec_imag = jnp.einsum(
        "kj,pwjc->pwkc", cos_grid, rot_imag, precision=lax.Precision.HIGHEST
    ) - jnp.einsum("kj,pwjc->pwkc", sin_grid, rot_real, precision=lax.Precision.HIGHEST)
    filt_real = spec_real[:, 0] * spec_real[:, 1] - spec_imag[:, 0] * spec_imag[:, 1]
    filt_imag = spec_real[:, 0] * spec_imag[:, 1] + spec_imag[:, 0] * spec_real[:, 1]
    back_real = jnp.einsum(
        "jk,pkc->pjc", cos_grid, filt_real, precision=lax.Precision.HIGHEST
    ) - jnp.einsum("jk,pkc->pjc", sin_grid, filt_imag, precision=lax.Precision.HIGHEST)
    back_imag = jnp.einsum(
        "jk,pkc->pjc", cos_grid, filt_imag, precision=lax.Precision.HIGHEST
    ) + jnp.einsum("jk,pkc->pjc", sin_grid, filt_real, precision=lax.Precision.HIGHEST)
    g_real, g_imag = rotate(back_real, back_imag, -twiddle[:, :, None])
    spectra = jnp.stack([g_real, g_imag], axis=1)
    for step_index in range(section_count):
        half_span = 1 << step_index
        partner = partner_2(spectra, "ctx", step_index)
        on_upper = my_index >> step_index & 1 == 1
        turn_angle = math.pi * (my_index & half_span - 1).astype(jnp.float32) / half_span
        own_real, own_imag = rotate(spectra[:, 0], spectra[:, 1], turn_angle)
        mate_real, mate_imag = rotate(partner[:, 0], partner[:, 1], turn_angle)
        lower_value = spectra + jnp.stack([mate_real, mate_imag], axis=1)
        upper_value = partner - jnp.stack([own_real, own_imag], axis=1)
        spectra = jnp.where(on_upper, upper_value, lower_value)
    last_turn = math.pi * my_index.astype(jnp.float32) / ctx_count
    odd_real, odd_imag = rotate(spectra[1, 0], spectra[1, 1], last_turn)
    long_conv = (spectra[0, 0] + odd_real) / spectrum_len
    return (q_feat * (long_conv + skip_gain[None, :] * product)).astype(jnp.bfloat16)


def solution(mesh):
    return jax.shard_map(
        body,
        mesh=mesh,
        in_specs=(P("ctx", "chan"), P("ctx"), P(None, "chan"), P("ctx", "chan"), P("chan")),
        out_specs=P("ctx", "chan"),
        check_vma=False,
    )
```

profile of v0, /device:TPU:1, one launch (start us, length us, event | category | flops | bytes accessed | tf_op | source)
XLA Modules:
  0.0 566.5 jit_solution(11479333067032492186)
XLA Ops:
  1.2 6.4 %scatter_fusion = s32[32,8]{0,1:T(8,128)S(1)} fusion(s32[32,8]{0,1:T(8,128)S(1)} %broadcast_in_dim.9, s32[128]{0:T(128)S(1)} %fusion.59, s32[128]{0:T(128)S(1)} %get-tuple-element.49), kind=kCustom, calls=%fused_computation | custom fusion | bytes 2560 | tf_op jit(solution)/shard_map/scatter | solution.py:49
  8.3 12.6 %all-to-all-start = ((s32[32,1,8]{2,1,0:T(1,128)}), s32[32,1,8]{2,1,0:T(1,128)S(1)}, u32[]{:S(2)}, u32[]{:S(2)}) async-start(s32[32,1,8]{2,1,0:T(1,128)} %copy.17), calls=%async_computation | async-start | bytes 32768 | tf_op jit(solution)/shard_map/all_to_all | solution.py:53
  20.9 1.0 broadcast_in_dim.11
  21.9 22.5 %scatter_fusion.1 = bf16[32,8,1536]{2,1,0:T(8,128)(2,1)} fusion(bf16[32,8,1536]{2,1,0:T(8,128)(2,1)} %broadcast_in_dim.11, s32[128]{0:T(128)S(1)} %fusion.59, bf16[128,1536]{1,0:T(8,128)(2,1)S(1)} %copy-done.15), kind=kCustom, calls=%fused_computation.1 | custom fusion | bytes 1180672 | tf_op jit(solution)/shard_map/scatter | solution.py:46
  44.4 10.2 %all-to-all-start.1 = ((bf16[32,8,1536]{2,1,0:T(8,128)(2,1)}), bf16[32,8,1536]{2,1,0:T(8,128)(2,1)S(1)}, u32[]{:S(2)}, u32[]{:S(2)}) async-start(bf16[32,8,1536]{2,1,0:T(8,128)(2,1)} %scatter_fusion.1), calls=%async_computation.1 | async-start | bytes 1572864 | tf_op jit(solution)/shard_map/all_to_all | solution.py:52
  55.8 22.1 %all-to-all-done.1 = bf16[32,8,1536]{2,1,0:T(8,128)(2,1)S(1)} async-done(((bf16[32,8,1536]{2,1,0:T(8,128)(2,1)}), bf16[32,8,1536]{2,1,0:T(8,128)(2,1)S(1)}, u32[]{:S(2)}, u32[]{:S(2)}) %all-to-all-start.1) | async-done | bytes 786464 | tf_op jit(solution)/shard_map/all_to_all | solution.py:52
  77.9 1.8 scatter_custom_fusion.2
  80.1 3.0 collective-permute-start
  83.7 4.2 collective-permute-done
  87.9 1.1 multiply_add_fusion.6
  90.1 1.5 pad_maximum_fusion
  91.6 4.0 collective-permute-start.1
  95.7 39.6 %collective-permute-done.1 = f32[2,2,2,128,512]{3,4,2,1,0:T(8,128)} collective-permute-done((f32[2,2,2,128,512]{3,4,2,1,0:T(8,128)}, f32[2,2,2,128,512]{3,4,2,1,0:T(8,128)}, u32[]{:S(2)}, u32[]{:S(2)}) %collective-permute-start.1) | collective-permute-done | bytes 2097184 | tf_op jit(solution)/shard_map/ppermute | solution.py:20
  135.3 1.8 fusion.96
  137.3 3.6 maximum_select_fusion
  141.0 4.1 collective-permute-start.2
  145.2 41.1 %collective-permute-done.2 = f32[2,2,2,128,512]{3,4,2,1,0:T(8,128)} collective-permute-done((f32[2,2,2,128,512]{3,4,2,1,0:T(8,128)}, f32[2,2,2,128,512]{3,4,2,1,0:T(8,128)}, u32[]{:S(2)}, u32[]{:S(2)}) %collective-permute-start.2) | collective-permute-done | bytes 2097184 | tf_op jit(solution)/shard_map/ppermute | solution.py:20
  186.3 2.9 fusion.101
  189.5 1.0 copy-done.2
  190.4 4.2 maximum_select_fusion.1
  194.7 5.1 collective-permute-start.3
  200.0 41.0 %collective-permute-done.3 = f32[2,2,2,128,512]{3,4,2,1,0:T(8,128)S(1)} collective-permute-done((f32[2,2,2,128,512]{3,4,2,1,0:T(8,128)}, f32[2,2,2,128,512]{3,4,2,1,0:T(8,128)S(1)}, u32[]{:S(2)}, u32[]{:S(2)}) %collective-permute-start.3) | collective-permute-done | bytes 2097184 | tf_op jit(solution)/shard_map/ppermute | solution.py:20
  240.9 2.6 sub.148
  243.7 2.5 maximum_select_fusion.2
  246.3 52.7 %collective-permute-start.4 = (f32[2,2,2,128,512]{3,4,2,1,0:T(8,128)S(1)}, f32[2,2,2,128,512]{3,4,2,1,0:T(8,128)}, u32[]{:S(2)}, u32[]{:S(2)}) collective-permute-start(f32[2,2,2,128,512]{3,4,2,1,0:T(8,128)S(1)} %maximum_select_fusion.2), channel_id=1, source_target_pairs={{0,16},{8,24},{16,0},{24,8},{32,48},{40,56},{48,32},{56,40},{64,80... | collective-permute-start | bytes 6291464 | tf_op jit(solution)/shard_map/ppermute | solution.py:20
  299.2 90.4 %collective-permute-done.4 = f32[2,2,2,128,512]{3,4,2,1,0:T(8,128)} collective-permute-done((f32[2,2,2,128,512]{3,4,2,1,0:T(8,128)S(1)}, f32[2,2,2,128,512]{3,4,2,1,0:T(8,128)}, u32[]{:S(2)}, u32[]{:S(2)}) %collective-permute-start.4) | collective-permute-done | bytes 2097184 | tf_op jit(solution)/shard_map/ppermute | solution.py:20
  389.6 1.8 sub.150
  391.6 2.5 maximum_select_fusion.3
  394.1 1.2 collective-permute-start.5
  395.4 3.8 collective-permute-done.5
  399.2 1.8 sub.152
  401.2 1.9 maximum_select_fusion.4
  403.1 1.2 fusion.26
  404.3 1.2 fusion.27
  405.5 1.2 fusion.1
  406.8 1.2 fusion
  410.6 0.9 fusion.11
  412.2 2.2 collective-permute-done.6
  414.5 1.3 fusion.2
  416.4 1.5 multiply_subtract_fusion.13
  417.8 46.3 %collective-permute-done.7 = f32[2,2,128,512]{2,3,0,1:T(8,128)S(1)} collective-permute-done((f32[2,2,128,512]{2,3,0,1:T(8,128)}, f32[2,2,128,512]{2,3,0,1:T(8,128)S(1)}, u32[]{:S(2)}, u32[]{:S(2)}) %collective-permute-start.7) | collective-permute-done | bytes 1048608 | tf_op jit(solution)/shard_map/ppermute | solution.py:20
  465.1 1.6 fusion.3
  466.7 5.2 collective-permute-start.8
  472.2 44.8 %collective-permute-done.8 = f32[2,2,128,512]{2,3,0,1:T(8,128)S(1)} collective-permute-done((f32[2,2,128,512]{2,3,0,1:T(8,128)S(1)}, f32[2,2,128,512]{2,3,0,1:T(8,128)S(1)}, u32[]{:S(2)}, u32[]{:S(2)}) %collective-permute-start.8) | collective-permute-done | bytes 1048608 | tf_op jit(solution)/shard_map/ppermute | solution.py:20
  517.4 1.4 collective-permute-start.9
  519.1 20.8 %collective-permute-done.9 = f32[2,2,128,512]{2,3,0,1:T(8,128)S(1)} collective-permute-done((f32[2,2,128,512]{2,3,0,1:T(8,128)S(1)}, f32[2,2,128,512]{2,3,0,1:T(8,128)S(1)}, u32[]{:S(2)}, u32[]{:S(2)}) %collective-permute-start.9) | collective-permute-done | bytes 1048608 | tf_op jit(solution)/shard_map/ppermute | solution.py:20
  540.4 3.4 collective-permute-start.10
  544.3 20.0 %collective-permute-done.10 = f32[2,2,128,512]{2,3,0,1:T(8,128)S(1)} collective-permute-done((f32[2,2,128,512]{2,3,0,1:T(8,128)S(1)}, f32[2,2,128,512]{2,3,0,1:T(8,128)S(1)}, u32[]{:S(2)}, u32[]{:S(2)}) %collective-permute-start.10) | collective-permute-done | bytes 1048608 | tf_op jit(solution)/shard_map/ppermute | solution.py:20
  (87 shorter events, 13.9 us)
Async XLA Ops:
  0.0 21.9 %copy-start.15 = (bf16[128,1536]{1,0:T(8,128)(2,1)S(1)}, bf16[128,1536]{1,0:T(8,128)(2,1)}, u32[]{:S(2)}) copy-start(bf16[128,1536]{1,0:T(8,128)(2,1)} %param.5) | copy-start | bytes 1179652
  8.3 36.1 %all-to-all-start = ((s32[32,1,8]{2,1,0:T(1,128)}), s32[32,1,8]{2,1,0:T(1,128)S(1)}, u32[]{:S(2)}, u32[]{:S(2)}) async-start(s32[32,1,8]{2,1,0:T(1,128)} %copy.17), calls=%async_computation | async-start | bytes 32768 | tf_op jit(solution)/shard_map/all_to_all | solution.py:53
  44.4 38.7 %copy-start.17 = (f32[3,1536]{1,0:T(4,128)S(1)}, f32[3,1536]{1,0:T(4,128)}, u32[]{:S(2)}) copy-start(f32[3,1536]{1,0:T(4,128)} %param.7) | copy-start | bytes 55300
  44.4 39.0 %copy-start.16 = (f32[128,512]{1,0:T(8,128)S(1)}, f32[128,512]{1,0:T(8,128)}, u32[]{:S(2)}) copy-start(f32[128,512]{1,0:T(8,128)} %param.8) | copy-start | bytes 786436
  44.4 33.5 %all-to-all-start.1 = ((bf16[32,8,1536]{2,1,0:T(8,128)(2,1)}), bf16[32,8,1536]{2,1,0:T(8,128)(2,1)S(1)}, u32[]{:S(2)}, u32[]{:S(2)}) async-start(bf16[32,8,1536]{2,1,0:T(8,128)(2,1)} %scatter_fusion.1), calls=%async_computation.1 | async-start | bytes 1572864 | tf_op jit(solution)/shard_map/all_to_all | solution.py:52
  80.1 7.8 %collective-permute-start = (bf16[2,1536]{0,1:T(8,128)(2,1)S(1)}, bf16[2,1536]{0,1:T(8,128)(2,1)S(1)}, u32[]{:S(2)}, u32[]{:S(2)}) collective-permute-start(bf16[2,1536]{0,1:T(8,128)(2,1)S(1)} %copy.19), channel_id=1, source_target_pairs={{0,8},{8,16},{16,24},{24,32},{32,40},{40,48},{48,56},{56,64},{64,7... | collective-permute-start | bytes 18440 | tf_op jit(solution)/shard_map/ppermute | solution.py:14
  89.0 1.0 copy-start.4
  91.6 43.7 %collective-permute-start.1 = (f32[2,2,2,128,512]{3,4,2,1,0:T(8,128)}, f32[2,2,2,128,512]{3,4,2,1,0:T(8,128)}, u32[]{:S(2)}, u32[]{:S(2)}) collective-permute-start(f32[2,2,2,128,512]{3,4,2,1,0:T(8,128)} %pad_maximum_fusion), channel_id=1, source_target_pairs={{0,128},{8,136},{16,144},{24,152},{32,160},{40,168},{48,176},{56,1... | collective-permute-start | bytes 6291464 | tf_op jit(solution)/shard_map/ppermute | solution.py:20
  137.3 3.7 copy-start.1
  141.0 45.4 %collective-permute-start.2 = (f32[2,2,2,128,512]{3,4,2,1,0:T(8,128)}, f32[2,2,2,128,512]{3,4,2,1,0:T(8,128)}, u32[]{:S(2)}, u32[]{:S(2)}) collective-permute-start(f32[2,2,2,128,512]{3,4,2,1,0:T(8,128)} %maximum_select_fusion), channel_id=1, source_target_pairs={{0,64},{8,72},{16,80},{24,88},{32,96},{40,104},{48,112},{56,120},{... | collective-permute-start | bytes 6291464 | tf_op jit(solution)/shard_map/ppermute | solution.py:20
  189.2 1.2 copy-start.2
  194.7 46.3 %collective-permute-start.3 = (f32[2,2,2,128,512]{3,4,2,1,0:T(8,128)}, f32[2,2,2,128,512]{3,4,2,1,0:T(8,128)S(1)}, u32[]{:S(2)}, u32[]{:S(2)}) collective-permute-start(f32[2,2,2,128,512]{3,4,2,1,0:T(8,128)} %maximum_select_fusion.1), channel_id=1, source_target_pairs={{0,32},{8,40},{16,48},{24,56},{32,0},{40,8},{48,16},{56,24},{64,96... | collective-permute-start | bytes 6291464 | tf_op jit(solution)/shard_map/ppermute | solution.py:20
  240.9 2.6 copy-start.3
  246.3 145.1 %copy-start = (f32[2,2,2,128,512]{3,4,2,1,0:T(8,128)}, f32[2,2,2,128,512]{3,4,2,1,0:T(8,128)S(1)}, u32[]{:S(2)}) copy-start(f32[2,2,2,128,512]{3,4,2,1,0:T(8,128)S(1)} %maximum_select_fusion.2) | copy-start | bytes 6291460
  246.3 143.3 %collective-permute-start.4 = (f32[2,2,2,128,512]{3,4,2,1,0:T(8,128)S(1)}, f32[2,2,2,128,512]{3,4,2,1,0:T(8,128)}, u32[]{:S(2)}, u32[]{:S(2)}) collective-permute-start(f32[2,2,2,128,512]{3,4,2,1,0:T(8,128)S(1)} %maximum_select_fusion.2), channel_id=1, source_target_pairs={{0,16},{8,24},{16,0},{24,8},{32,48},{40,56},{48,32},{56,40},{64,80... | collective-permute-start | bytes 6291464 | tf_op jit(solution)/shard_map/ppermute | solution.py:20
  394.1 5.1 collective-permute-start.5
  411.6 2.9 copy-start.8
  411.6 2.8 collective-permute-start.6
  412.2 3.7 copy-start.6
  414.5 1.4 copy-start.10
  414.5 1.4 copy-start.12
  415.9 48.3 %collective-permute-start.7 = (f32[2,2,128,512]{2,3,0,1:T(8,128)}, f32[2,2,128,512]{2,3,0,1:T(8,128)S(1)}, u32[]{:S(2)}, u32[]{:S(2)}) collective-permute-start(f32[2,2,128,512]{2,3,0,1:T(8,128)} %fusion.2), channel_id=1, source_target_pairs={{0,16},{8,24},{16,0},{24,8},{32,48},{40,56},{48,32},{56,40},{64,80... | collective-permute-start | bytes 3145736 | tf_op jit(solution)/shard_map/ppermute | solution.py:20
  416.3 48.8 %copy-start.7 = (f32[2,1,128,512]{2,3,0,1:T(8,128)S(1)}, f32[2,1,128,512]{2,3,0,1:T(8,128)}, u32[]{:S(2)}) copy-start(f32[2,1,128,512]{2,3,0,1:T(8,128)} %copy-done.6) | copy-start | bytes 1572868
  416.3 48.8 %copy-start.9 = (f32[2,1,128,512]{2,3,0,1:T(8,128)S(1)}, f32[2,1,128,512]{2,3,0,1:T(8,128)}, u32[]{:S(2)}) copy-start(f32[2,1,128,512]{2,3,0,1:T(8,128)} %copy-done.8) | copy-start | bytes 1572868
  416.3 48.8 %copy-start.11 = (f32[2,1,128,512]{2,3,0,1:T(8,128)S(1)}, f32[2,1,128,512]{2,3,0,1:T(8,128)}, u32[]{:S(2)}) copy-start(f32[2,1,128,512]{2,3,0,1:T(8,128)} %copy-done.10) | copy-start | bytes 1572868
  416.4 48.7 %copy-start.13 = (f32[2,1,128,512]{2,3,0,1:T(8,128)S(1)}, f32[2,1,128,512]{2,3,0,1:T(8,128)}, u32[]{:S(2)}) copy-start(f32[2,1,128,512]{2,3,0,1:T(8,128)} %copy-done.12) | copy-start | bytes 1572868
  464.1 1.0 copy-start.14
  466.7 50.3 %collective-permute-start.8 = (f32[2,2,128,512]{2,3,0,1:T(8,128)S(1)}, f32[2,2,128,512]{2,3,0,1:T(8,128)S(1)}, u32[]{:S(2)}, u32[]{:S(2)}) collective-permute-start(f32[2,2,128,512]{2,3,0,1:T(8,128)S(1)} %fusion.3), channel_id=1, source_target_pairs={{0,32},{8,40},{16,48},{24,56},{32,0},{40,8},{48,16},{56,24},{64,96... | collective-permute-start | bytes 3145736 | tf_op jit(solution)/shard_map/ppermute | solution.py:20
  517.4 22.6 %collective-permute-start.9 = (f32[2,2,128,512]{2,3,0,1:T(8,128)S(1)}, f32[2,2,128,512]{2,3,0,1:T(8,128)S(1)}, u32[]{:S(2)}, u32[]{:S(2)}) collective-permute-start(f32[2,2,128,512]{2,3,0,1:T(8,128)S(1)} %fusion.4), channel_id=1, source_target_pairs={{0,64},{8,72},{16,80},{24,88},{32,96},{40,104},{48,112},{56,120},{... | collective-permute-start | bytes 3145736 | tf_op jit(solution)/shard_map/ppermute | solution.py:20
  540.4 23.9 %collective-permute-start.10 = (f32[2,2,128,512]{2,3,0,1:T(8,128)S(1)}, f32[2,2,128,512]{2,3,0,1:T(8,128)S(1)}, u32[]{:S(2)}, u32[]{:S(2)}) collective-permute-start(f32[2,2,128,512]{2,3,0,1:T(8,128)S(1)} %fusion.5), channel_id=1, source_target_pairs={{0,128},{8,136},{16,144},{24,152},{32,160},{40,168},{48,176},{56,1... | collective-permute-start | bytes 3145736 | tf_op jit(solution)/shard_map/ppermute | solution.py:20
  564.4 1.1 copy-start.5
  564.4 1.1 copy-start.18
where the time goes:
time: 570 us; the launch traced here: 566 us
  waiting for transfers between devices  376 us (66%)
  starting transfers between devices  104 us (18%)
  local copies, waits for them, and re-layouts  38 us (7%)
  other arithmetic  38 us (7%)
  matrix products  8.31 us (1%)
    ppermute x10, waiting for transfers between devices, partner_2(): return lax.ppermute(value, axis, pairs)  350 us
    ppermute x10, starting transfers between devices, partner_2(): return lax.ppermute(value, axis, pairs)  78 us
    scatter x1, local copies, waits for them, and re-layouts, body(): outgoing = jnp.zeros((ctx_count, capacity, loader_rows.shape[1]), loader_...  22.5 us
    all_to_all x1, waiting for transfers between devices, body(): lax.all_to_all(outgoing, 'ctx', split_axis=0, concat_axis=0, tiled=True)  22.1 us
    select_n x10, other arithmetic, body(): spectra = jnp.where(on_upper, upper_value, lower_value)  18.6 us
    all_to_all x1, starting transfers between devices, body(): lax.all_to_all(targets, 'ctx', split_axis=0, concat_axis=0, tiled=True)  12.6 us
  transfers between devices with their start and end apart: 13, of which 12 were waited for; matrix products, arithmetic and copies ran while one was open for 5% of the time, Pallas kernels for 0%

commit v1 on v0

v1 whole, which is shorter than its diff:
```python
import functools
import math

import jax
import jax.numpy as jnp
import ml_dtypes
import numpy as np
from jax import lax
from jax.experimental import pallas as pl
from jax.experimental.pallas import tpu as pltpu
from jax.sharding import PartitionSpec as P

N = 32
B = 128
C = 16
W = 512
CAP = 8
F32, BF16 = jnp.float32, jnp.bfloat16
NT = (((1,), (1,)), ((), ()))
TN = (((0,), (0,)), ((), ()))
NN = (((1,), (0,)), ((), ()))


def dot(a, b, dims=NN):
    return lax.dot_general(a, b, dims, preferred_element_type=F32)


def halves(x):
    hi = x.astype(BF16)
    return hi, (x - hi.astype(F32)).astype(BF16)


def np_halves(x):
    hi = x.astype(ml_dtypes.bfloat16)
    return hi, (x - hi.astype(np.float64)).astype(ml_dtypes.bfloat16)


@functools.cache
def tables():
    quarter = np.arange(N) + 0.25
    block = 2 * math.pi * np.outer(quarter, np.arange(N)) / N
    turn = 2 * math.pi * np.outer(quarter, np.arange(B)) / (N * B)
    lane = 2 * math.pi * (np.outer(np.arange(B), np.arange(B)) % B) / B
    hi, lo = np_halves(np.concatenate([np.cos(block), -np.sin(block)]))
    first = np.concatenate([hi, hi, lo], axis=1)
    hi, lo = np_halves(np.concatenate([np.cos(block.T), -np.sin(block.T)], axis=1) / (N * B))
    last = np.concatenate([hi, hi, lo], axis=1)
    twiddle = np.stack([np.cos(turn), np.sin(turn)]).astype(np.float32)
    c, s = np.cos(lane), np.sin(lane)
    fwd = np.stack(np_halves(np.block([[c, -s], [s, c]])))
    inv = np.stack(np_halves(np.block([[c, s], [-s, c]])))
    return first, twiddle, fwd, inv, last


def iota(shape, dim):
    return lax.broadcasted_iota(jnp.int32, shape, dim)


def wide(z, g_ref):
    hi, lo = halves(z)
    return dot(hi, g_ref[0]) + (dot(lo, g_ref[0]) + dot(hi, g_ref[1]))


def forward(src, first_ref, tw_ref, fwd_ref, dst):
    cos, sin = tw_ref[0], tw_ref[1]
    first = first_ref[...]
    for c in range(C):
        hi, lo = halves(src[pl.ds(c, N, C), :])
        y = dot(first, jnp.concatenate([hi, lo, hi], axis=0))
        re, im = y[:N], y[N:]
        dst[pl.ds(c * N, N), :] = jnp.concatenate(
            [re * cos + im * sin, im * cos - re * sin], axis=1
        )
    dst[...] = wide(dst[...], fwd_ref)


def kernel(
    rows_ref, pos_ref, w_ref, filt_ref, gain_ref, first_ref, tw_ref, fwd_ref, inv_ref, last_ref,
    out_ref,
    x_send, f_send, code_send, x_recv, f_recv, code_recv, onehot, place, cand,
    q_feat, prod, spec_p, spec_f, conv, o_send, o_recv,
    send_sems, recv_sems,
):
    me = lax.axis_index("ctx")
    barrier = pltpu.get_barrier_semaphore()

    def greet(k, _):
        pl.semaphore_signal(
            barrier,
            inc=1,
            device_id={"ctx": lax.rem(me + k, N)},
            device_id_type=pl.DeviceIdType.MESH,
        )
        return 0

    lax.fori_loop(1, N, greet, 0)

    pos = pos_ref[...]
    owner = pos // B
    across = jnp.broadcast_to(owner.astype(F32), (B, B))
    down = across.T
    earlier = (across == down) & (iota((B, B), 0) < iota((B, B), 1))
    rank = jnp.sum(jnp.where(earlier, 1.0, 0.0), axis=0, keepdims=True).astype(jnp.int32)
    code = (owner * CAP + rank) * B + (pos - owner * B)
    code_send[...] = code
    code_recv[me] = code

    per = B // C
    for part in range(3):
        for j in range(W // B):
            chunk = rows_ref[:, part * W + j * B : part * W + (j + 1) * B].T
            x_send[j * per : (j + 1) * per, part * C : (part + 1) * C, :] = chunk.reshape(per, C, B)
    for j in range(W // B):
        f_send[j * B : (j + 1) * B, :] = filt_ref[:, j * B : (j + 1) * B].T
    x_recv[me] = x_send[me]
    mine = pl.ds(pl.multiple_of(me * C, C), C)
    f_recv[mine, :] = f_send[mine, :]

    pl.semaphore_wait(barrier, N - 1)

    def copy(src, dst, i, to):
        return pltpu.make_async_remote_copy(
            src_ref=src,
            dst_ref=dst,
            send_sem=send_sems.at[i],
            recv_sem=recv_sems.at[i],
            device_id={"ctx": to},
            device_id_type=pl.DeviceIdType.MESH,
        )

    def send_code(k, _):
        copy(code_send, code_recv.at[me], 0, lax.rem(me + k, N)).start()
        return 0

    def send_rows(k, _):
        to = lax.rem(me + k, N)
        copy(x_send.at[to], x_recv.at[me], 1, to).start()
        return 0

    def send_filter(k, _):
        to = lax.rem(me + k, N)
        theirs = pl.ds(pl.multiple_of(to * C, C), C)
        copy(f_send.at[theirs, :], f_recv.at[mine, :], 2, to).start()
        return 0

    lax.fori_loop(1, N, send_code, 0)
    lax.fori_loop(1, N, send_rows, 0)
    lax.fori_loop(1, N, send_filter, 0)

    def arrived(buf, i, count):
        part = buf.at[pl.ds(0, count)]
        pltpu.make_async_copy(part, part, recv_sems.at[i]).wait()

    def left(buf, i, count):
        part = buf.at[pl.ds(0, count)]
        pltpu.make_async_copy(part, part, send_sems.at[i]).wait()

    pick = iota((C, W), 1) == me * C + iota((C, W), 0)

    def column(row):
        return jnp.sum(jnp.where(pick, row, 0.0), axis=1, keepdims=True)

    taps = [
        jnp.concatenate([column(w_ref[i : i + 1, p * W : (p + 1) * W]) for p in range(3)], axis=0)
        for i in range(3)
    ]
    gain = column(gain_ref[...])

    arrived(code_recv, 0, N - 1)

    def index(h, _):
        tiles = []
        for s in (2 * h, 2 * h + 1):
            code = code_recv[s]
            slot = code // B
            within = (code - slot * B + 1).astype(F32)
            hot = (iota((N * CAP, B), 0) == slot).astype(F32).astype(BF16)
            onehot[s] = hot
            at = dot(hot, jnp.broadcast_to(within, (B, B)).astype(BF16), NT)
            tile = (at == (iota((N * CAP, B), 1) + 1).astype(F32)).astype(F32)
            tiles.append(tile.reshape(N, CAP, B))
        both = jnp.concatenate(tiles, axis=1).astype(BF16)
        place[:, pl.ds(pl.multiple_of(h * 2 * CAP, 2 * CAP), 2 * CAP), :] = both
        return 0

    lax.fori_loop(0, N // 2, index, 0)

    arrived(x_recv, 1, N - 1)

    def spread(h, _):
        tiles = [
            dot(onehot[s], x_recv[s], NT).reshape(N, CAP, 3 * C) for s in (2 * h, 2 * h + 1)
        ]
        both = jnp.concatenate(tiles, axis=1).astype(BF16)
        cand[:, pl.ds(pl.multiple_of(h * 2 * CAP, 2 * CAP), 2 * CAP), :] = both
        return 0

    lax.fori_loop(0, N // 2, spread, 0)

    lane = iota((3 * C, B), 1)

    def block(o, before):
        seq = dot(cand[o], place[o], TN)
        feat = taps[0] * seq
        for i in (1, 2):
            moved = jnp.where(lane < i, pltpu.roll(before, i, 1), pltpu.roll(seq, i, 1))
            feat = feat + taps[i] * moved
        here = pl.ds(pl.multiple_of(o * C, C), C)
        q_feat[here, :] = feat[:C]
        prod[here, :] = feat[C : 2 * C] * feat[2 * C :]
        return seq

    lax.fori_loop(0, N, block, jnp.zeros((3 * C, B), F32))

    forward(prod, first_ref, tw_ref, fwd_ref, spec_p)
    arrived(f_recv, 2, (N - 1) * C)
    forward(f_recv, first_ref, tw_ref, fwd_ref, spec_f)

    a_re, a_im = spec_p[:, :B], spec_p[:, B:]
    b_re, b_im = spec_f[:, :B], spec_f[:, B:]
    z = jnp.concatenate([a_re * b_re - a_im * b_im, a_re * b_im + a_im * b_re], axis=1)
    spec_p[...] = wide(z, inv_ref)
    cos, sin = tw_ref[0], tw_ref[1]
    last = last_ref[...]
    for c in range(C):
        y = spec_p[pl.ds(c * N, N), :]
        re, im = y[:, :B], y[:, B:]
        hi, lo = halves(jnp.concatenate([re * cos - im * sin, im * cos + re * sin], axis=0))
        conv[pl.ds(c, N, C), :] = dot(last, jnp.concatenate([hi, lo, hi], axis=0))

    def finish(k, _):
        to = lax.rem(me + k, N)
        theirs = pl.ds(pl.multiple_of(to * C, C), C)
        value = q_feat[theirs, :] * (conv[theirs, :] + gain * prod[theirs, :])
        o_send[theirs, :] = value.astype(BF16)

        @pl.when(k < N)
        def _():
            copy(o_send.at[theirs, :], o_recv.at[mine, :], 3, to).start()

        return 0

    lax.fori_loop(1, N + 1, finish, 0)
    o_recv[mine, :] = o_send[mine, :]

    left(code_recv, 0, N - 1)
    left(x_send, 1, N - 1)
    left(f_send, 2, (N - 1) * C)
    left(o_send, 3, (N - 1) * C)
    arrived(o_recv, 3, (N - 1) * C)
    for j in range(W // B):
        out_ref[:, j * B : (j + 1) * B] = o_recv[j * B : (j + 1) * B, :].T


def body(loader_rows, row_pos, short_w, long_filter, skip_gain):
    consts = [jnp.asarray(t) for t in tables()]
    vmem = pl.BlockSpec(memory_space=pltpu.VMEM)
    return pl.pallas_call(
        kernel,
        out_shape=jax.ShapeDtypeStruct((B, W), BF16),
        in_specs=[vmem] * 10,
        out_specs=vmem,
        scratch_shapes=[
            pltpu.VMEM((N, 3 * C, B), BF16),
            pltpu.VMEM((W, B), F32),
            pltpu.VMEM((1, B), jnp.int32),
            pltpu.VMEM((N, 3 * C, B), BF16),
            pltpu.VMEM((W, B), F32),
            pltpu.VMEM((N, 1, B), jnp.int32),
            pltpu.VMEM((N, N * CAP, B), BF16),
            pltpu.VMEM((N, N * CAP, B), BF16),
            pltpu.VMEM((N, N * CAP, 3 * C), BF16),
            pltpu.VMEM((W, B), F32),
            pltpu.VMEM((W, B), F32),
            pltpu.VMEM((W, 2 * B), F32),
            pltpu.VMEM((W, 2 * B), F32),
            pltpu.VMEM((W, B), F32),
            pltpu.VMEM((W, B), BF16),
            pltpu.VMEM((W, B), BF16),
            pltpu.SemaphoreType.DMA((4,)),
            pltpu.SemaphoreType.DMA((4,)),
        ],
        compiler_params=pltpu.CompilerParams(
            collective_id=0, has_side_effects=True, vmem_limit_bytes=48 << 20
        ),
    )(loader_rows, row_pos.reshape(1, B), short_w, long_filter, skip_gain.reshape(1, W), *consts)


def solution(mesh):
    return jax.shard_map(
        body,
        mesh=mesh,
        in_specs=(P("ctx", "chan"), P("ctx"), P(None, "chan"), P("ctx", "chan"), P("chan")),
        out_specs=P("ctx", "chan"),
        check_vma=False,
    )
```

time: 570 us -> 51.9 us (0.09)
  waiting for transfers between devices: 376 us -> 0 us
  starting transfers between devices: 104 us -> 0 us
  Pallas kernels: 0 us -> 43.3 us
  other arithmetic: 38 us -> 0 us
  local copies, waits for them, and re-layouts: 38 us -> 8.11 us
  matrix products: 8.31 us -> 0 us
    ppermute x11 -> x0, waiting for transfers between devices: 354 us -> none  [the longest x10 350 us: partner_2(): return lax.ppermute(value, axis, pairs)]
    ppermute x11 -> x0, starting transfers between devices: 81 us -> none  [the longest x10 78 us: partner_2(): return lax.ppermute(value, axis, pairs)]
    pallas_call x0 -> x1, Pallas kernels: none -> 43.3 us  [body(): pl.pallas_call(kernel, out_shape=jax.ShapeDtypeStruct((B, W), BF16), in_s...]
    scatter x3 -> x0, local copies, waits for them, and re-layouts: 30.8 us -> none  [the longest x1 22.5 us: body(): outgoing = jnp.zeros((ctx_count, capacity, loader_rows.shape[1]), loader_...]
    all_to_all x2 -> x0, starting transfers between devices: 22.7 us -> none  [the longest x1 12.6 us: body(): lax.all_to_all(targets, 'ctx', split_axis=0, concat_axis=0, tiled=True)]
    all_to_all x2 -> x0, waiting for transfers between devices: 22.1 us -> none  [the longest x1 22.1 us: body(): lax.all_to_all(outgoing, 'ctx', split_axis=0, concat_axis=0, tiled=True)]
    select_n x12 -> x0, other arithmetic: 19.3 us -> none  [the longest x10 18.6 us: body(): spectra = jnp.where(on_upper, upper_value, lower_value)]
    sub x21 -> x0, other arithmetic: 14.4 us -> none  [the longest x5 10.9 us: body(): difference = partner - spectra]
  transfers between devices with their start and end apart: 13 -> 0, of which waited for: 12 -> 0; matrix products, arithmetic and copies ran while one was open for 5% -> 0% of each run, Pallas kernels for 0% -> 0%
where the time goes in v1:
time: 51.9 us; the launch traced here: 51.5 us
  Pallas kernels  43.3 us (83%)
  local copies, waits for them, and re-layouts  8.11 us (16%)
    pallas_call x1, Pallas kernels, body(): pl.pallas_call(kernel, out_shape=jax.ShapeDtypeStruct((B, W), BF16), in_s...  43.3 us
    unnamed x21, local copies, waits for them, and re-layouts  8.11 us

profile of v1, /device:TPU:1, one launch (start us, length us, event | category | flops | bytes accessed | tf_op | source)
XLA Modules:
  0.0 51.5 jit_solution(4591985461111546973)
XLA Ops:
  0.0 0.0 copy-start.8
  0.0 0.0 copy-start.9
  0.0 0.7 %copy-done.8 = f32[512]{0:T(512)S(1)} copy-done((f32[512]{0:T(512)S(1)}, f32[512]{0:T(512)}, u32[]{:S(2)}) %copy-start.8) | copy-done | bytes 2072
  0.7 0.0 copy-done.9
  0.7 0.0 copy-start
  0.7 1.0 %copy-done = bf16[128,1536]{1,0:T(8,128)(2,1)S(1)} copy-done((bf16[128,1536]{1,0:T(8,128)(2,1)S(1)}, bf16[128,1536]{1,0:T(8,128)(2,1)}, u32[]{:S(2)}) %copy-start) | copy-done | bytes 393240
  1.7 0.0 copy-start.1
  1.7 0.9 %copy-done.1 = f32[128,512]{1,0:T(8,128)S(1)} copy-done((f32[128,512]{1,0:T(8,128)S(1)}, f32[128,512]{1,0:T(8,128)}, u32[]{:S(2)}) %copy-start.1) | copy-done | bytes 262168
  2.6 0.0 copy-start.2
  2.6 0.9 %copy-done.2 = bf16[2,256,256]{2,1,0:T(8,128)(2,1)S(1)} copy-done((bf16[2,256,256]{2,1,0:T(8,128)(2,1)S(1)}, bf16[2,256,256]{2,1,0:T(8,128)(2,1)}, u32[]{:S(2)}) %copy-start.2) | copy-done | bytes 262168
  3.6 0.0 copy-start.3
  3.6 0.9 %copy-done.3 = bf16[2,256,256]{2,1,0:T(8,128)(2,1)S(1)} copy-done((bf16[2,256,256]{2,1,0:T(8,128)(2,1)S(1)}, bf16[2,256,256]{2,1,0:T(8,128)(2,1)}, u32[]{:S(2)}) %copy-start.3) | copy-done | bytes 262168
  4.5 0.0 copy-start.4
  4.5 0.8 %copy-done.4 = f32[2,32,128]{2,1,0:T(8,128)S(1)} copy-done((f32[2,32,128]{2,1,0:T(8,128)S(1)}, f32[2,32,128]{2,1,0:T(8,128)}, u32[]{:S(2)}) %copy-start.4) | copy-done | bytes 32792
  5.3 0.0 copy-start.5
  5.3 0.7 %copy-done.5 = f32[3,1536]{1,0:T(4,128)S(1)} copy-done((f32[3,1536]{1,0:T(4,128)S(1)}, f32[3,1536]{1,0:T(4,128)}, u32[]{:S(2)}) %copy-start.5) | copy-done | bytes 18456
  6.0 0.0 copy-start.6
  6.0 0.7 %copy-done.6 = bf16[32,192]{1,0:T(8,128)(2,1)S(1)} copy-done((bf16[32,192]{1,0:T(8,128)(2,1)S(1)}, bf16[32,192]{1,0:T(8,128)(2,1)}, u32[]{:S(2)}) %copy-start.6) | copy-done | bytes 12312
  6.7 0.0 copy-start.7
  6.8 0.7 %copy-done.7 = bf16[64,96]{1,0:T(8,128)(2,1)S(1)} copy-done((bf16[64,96]{1,0:T(8,128)(2,1)S(1)}, bf16[64,96]{1,0:T(8,128)(2,1)}, u32[]{:S(2)}) %copy-start.7) | copy-done | bytes 12312
  7.5 43.3 %shard_map.100 = bf16[128,512]{1,0:T(8,128)(2,1)S(1)} custom-call(bf16[128,1536]{1,0:T(8,128)(2,1)S(1)} %copy-done, s32[1,128]{1,0:T(1,128)S(1)} %bitcast.3, f32[3,1536]{1,0:T(4,128)S(1)} %copy-done.5, f32[128,512]{1,0:T(8,128)S(1)} %copy-done.1, f32[1,512]{1,0:T(1,128)S(1)} %bitcast.2, bf16[64,96]{1,0:T(8,128)(2,1)S(1)} %copy-done.7, ...), custom_call_target="tpu_custom_call" | custom-call | tf_op jit(solution)/shard_map/pallas_call | solution.py:258
  50.8 0.7 %copy.12 = bf16[128,512]{1,0:T(8,128)(2,1)} copy(bf16[128,512]{1,0:T(8,128)(2,1)S(1)} %shard_map.100) | data formatting | bytes 262144
Async XLA Ops:
  0.0 0.7 %copy-start.8 = (f32[512]{0:T(512)S(1)}, f32[512]{0:T(512)}, u32[]{:S(2)}) copy-start(f32[512]{0:T(512)} %param.14) | copy-start | bytes 6148
  0.0 0.7 %copy-start.9 = (s32[128]{0:T(128)S(1)}, s32[128]{0:T(128)}, u32[]{:S(2)}) copy-start(s32[128]{0:T(128)} %param.11) | copy-start | bytes 1540
  0.7 1.0 %copy-start = (bf16[128,1536]{1,0:T(8,128)(2,1)S(1)}, bf16[128,1536]{1,0:T(8,128)(2,1)}, u32[]{:S(2)}) copy-start(bf16[128,1536]{1,0:T(8,128)(2,1)} %rows_ref.1) | copy-start | bytes 1179652
  1.7 0.9 %copy-start.1 = (f32[128,512]{1,0:T(8,128)S(1)}, f32[128,512]{1,0:T(8,128)}, u32[]{:S(2)}) copy-start(f32[128,512]{1,0:T(8,128)} %filt_ref.1) | copy-start | bytes 786436
  2.6 0.9 %copy-start.2 = (bf16[2,256,256]{2,1,0:T(8,128)(2,1)S(1)}, bf16[2,256,256]{2,1,0:T(8,128)(2,1)}, u32[]{:S(2)}) copy-start(bf16[2,256,256]{2,1,0:T(8,128)(2,1)} %constant.13.clone.inv_ref) | copy-start | bytes 786436
  3.6 0.9 %copy-start.3 = (bf16[2,256,256]{2,1,0:T(8,128)(2,1)S(1)}, bf16[2,256,256]{2,1,0:T(8,128)(2,1)}, u32[]{:S(2)}) copy-start(bf16[2,256,256]{2,1,0:T(8,128)(2,1)} %constant.12.clone.fwd_ref) | copy-start | bytes 786436
  4.5 0.8 %copy-start.4 = (f32[2,32,128]{2,1,0:T(8,128)S(1)}, f32[2,32,128]{2,1,0:T(8,128)}, u32[]{:S(2)}) copy-start(f32[2,32,128]{2,1,0:T(8,128)} %constant.11.clone.tw_ref) | copy-start | bytes 98308
  5.3 0.7 %copy-start.5 = (f32[3,1536]{1,0:T(4,128)S(1)}, f32[3,1536]{1,0:T(4,128)}, u32[]{:S(2)}) copy-start(f32[3,1536]{1,0:T(4,128)} %w_ref.1) | copy-start | bytes 55300
  6.0 0.7 %copy-start.6 = (bf16[32,192]{1,0:T(8,128)(2,1)S(1)}, bf16[32,192]{1,0:T(8,128)(2,1)}, u32[]{:S(2)}) copy-start(bf16[32,192]{1,0:T(8,128)(2,1)} %constant.14.clone.last_ref) | copy-start | bytes 36868
  6.7 0.7 %copy-start.7 = (bf16[64,96]{1,0:T(8,128)(2,1)S(1)}, bf16[64,96]{1,0:T(8,128)(2,1)}, u32[]{:S(2)}) copy-start(bf16[64,96]{1,0:T(8,128)(2,1)} %constant.10.clone.first_ref) | copy-start | bytes 36868

commit v2 on v1

--- a/solution.py
+++ b/solution.py
@@ -14,6 +14,7 @@
 B = 128
 C = 16
 W = 512
+ARGS = 10
 CAP = 8
 F32, BF16 = jnp.float32, jnp.bfloat16
 NT = (((1,), (1,)), ((), ()))
@@ -75,7 +76,21 @@
 
 
 def kernel(
-    rows_ref, pos_ref, w_ref, filt_ref, gain_ref, first_ref, tw_ref, fwd_ref, inv_ref, last_ref,
+    *refs,
+):
+    given, out_ref, here = refs[:ARGS], refs[ARGS], refs[ARGS + 1 : 2 * ARGS + 1]
+    scratch, load_sems = refs[2 * ARGS + 1 : -1], refs[-1]
+    loads = [
+        pltpu.make_async_copy(given[i], here[i], load_sems.at[i]) for i in range(ARGS)
+    ]
+    for load in loads:
+        load.start()
+    work(loads, *here, out_ref, *scratch)
+
+
+def work(
+    loads,
+    pos_ref, rows_ref, filt_ref, w_ref, gain_ref, first_ref, tw_ref, last_ref, fwd_ref, inv_ref,
     out_ref,
     x_send, f_send, code_send, x_recv, f_recv, code_recv, onehot, place, cand,
     q_feat, prod, spec_p, spec_f, conv, o_send, o_recv,
@@ -95,6 +110,7 @@
 
     lax.fori_loop(1, N, greet, 0)
 
+    loads[0].wait()
     pos = pos_ref[...]
     owner = pos // B
     across = jnp.broadcast_to(owner.astype(F32), (B, B))
@@ -105,11 +121,13 @@
     code_send[...] = code
     code_recv[me] = code
 
+    loads[1].wait()
     per = B // C
     for part in range(3):
         for j in range(W // B):
             chunk = rows_ref[:, part * W + j * B : part * W + (j + 1) * B].T
             x_send[j * per : (j + 1) * per, part * C : (part + 1) * C, :] = chunk.reshape(per, C, B)
+    loads[2].wait()
     for j in range(W // B):
         f_send[j * B : (j + 1) * B, :] = filt_ref[:, j * B : (j + 1) * B].T
     x_recv[me] = x_send[me]
@@ -154,6 +172,9 @@
     def left(buf, i, count):
         part = buf.at[pl.ds(0, count)]
         pltpu.make_async_copy(part, part, send_sems.at[i]).wait()
+
+    for load in loads[3:]:
+        load.wait()
 
     pick = iota((C, W), 1) == me * C + iota((C, W), 0)
 
@@ -253,14 +274,18 @@
 
 
 def body(loader_rows, row_pos, short_w, long_filter, skip_gain):
-    consts = [jnp.asarray(t) for t in tables()]
-    vmem = pl.BlockSpec(memory_space=pltpu.VMEM)
+    first, twiddle, fwd, inv, last = (jnp.asarray(t) for t in tables())
+    operands = [
+        row_pos.reshape(1, B), loader_rows, long_filter, short_w, skip_gain.reshape(1, W),
+        first, twiddle, last, fwd, inv,
+    ]
     return pl.pallas_call(
         kernel,
         out_shape=jax.ShapeDtypeStruct((B, W), BF16),
-        in_specs=[vmem] * 10,
-        out_specs=vmem,
+        in_specs=[pl.BlockSpec(memory_space=pltpu.HBM)] * ARGS,
+        out_specs=pl.BlockSpec(memory_space=pltpu.VMEM),
         scratch_shapes=[
+            *(pltpu.VMEM(x.shape, x.dtype) for x in operands),
             pltpu.VMEM((N, 3 * C, B), BF16),
             pltpu.VMEM((W, B), F32),
             pltpu.VMEM((1, B), jnp.int32),
@@ -279,11 +304,12 @@
             pltpu.VMEM((W, B), BF16),
             pltpu.SemaphoreType.DMA((4,)),
             pltpu.SemaphoreType.DMA((4,)),
+            pltpu.SemaphoreType.DMA((ARGS,)),
         ],
         compiler_params=pltpu.CompilerParams(
-            collective_id=0, has_side_effects=True, vmem_limit_bytes=48 << 20
+            collective_id=0, has_side_effects=True, vmem_limit_bytes=60 << 20
         ),
-    )(loader_rows, row_pos.reshape(1, B), short_w, long_filter, skip_gain.reshape(1, W), *consts)
+    )(*operands)
 
 
 def solution(mesh):

time: 51.9 us -> 46.2 us (0.89)
  local copies, waits for them, and re-layouts: 8.11 us -> 1.57 us
  Pallas kernels: 43.3 us -> 44.5 us
    unnamed x21 -> x1, local copies, waits for them, and re-layouts: 8.11 us -> 1.57 us
    pallas_call x1, Pallas kernels: 43.3 us -> 44.5 us  [body(): pl.pallas_call(kernel, out_shape=jax.ShapeDtypeStruct((B, W), BF16), in_s...]
where the time goes in v2:
time: 46.2 us; the launch traced here: 46.1 us
  Pallas kernels  44.5 us (96%)
  local copies, waits for them, and re-layouts  1.57 us (3%)
    pallas_call x1, Pallas kernels, body(): pl.pallas_call(kernel, out_shape=jax.ShapeDtypeStruct((B, W), BF16), in_s...  44.5 us
    unnamed x1, local copies, waits for them, and re-layouts  1.57 us

profile of v2, /device:TPU:1, one launch (start us, length us, event | category | flops | bytes accessed | tf_op | source)
XLA Modules:
  0.0 46.1 jit_solution(15276041703611141236)
XLA Ops:
  0.0 44.5 %shard_map.100 = bf16[128,512]{1,0:T(8,128)(2,1)} custom-call(s32[1,128]{1,0:T(1,128)} %bitcast.3, bf16[128,1536]{1,0:T(8,128)(2,1)} %refs_1_.1, f32[128,512]{1,0:T(8,128)} %refs_2_.1, f32[3,1536]{1,0:T(4,128)} %refs_3_.1, f32[1,512]{1,0:T(1,128)} %bitcast.2, bf16[64,96]{1,0:T(8,128)(2,1)} %constant.10.clone.refs_5_, f32[2,32,128]{2,1,0:T(8,128)} %constant.11.clone.refs_6_, ...), custom_call_target="tpu_custom_call" | custom-call | tf_op jit(solution)/shard_map/pallas_call | solution.py:282
  44.5 1.6 %copy.12 = bf16[128,512]{1,0:T(8,128)(2,1)} copy(bf16[128,512]{1,0:T(8,128)(2,1)} %shard_map.100) | data formatting | bytes 262144

commit v3 on v2

v3 whole, which is shorter than its diff:
```python
import functools
import math

import jax
import jax.numpy as jnp
import ml_dtypes
import numpy as np
from jax import lax
from jax.experimental import pallas as pl
from jax.experimental.pallas import tpu as pltpu
from jax.sharding import PartitionSpec as P

N = 32
B = 128
C = 16
W = 512
ARGS = 10
STEPS = 32767.0
CAP = 8
F32, BF16 = jnp.float32, jnp.bfloat16
NT = (((1,), (1,)), ((), ()))
TN = (((0,), (0,)), ((), ()))
NN = (((1,), (0,)), ((), ()))


def dot(a, b, dims=NN):
    return lax.dot_general(a, b, dims, preferred_element_type=F32)


def halves(x):
    hi = x.astype(BF16)
    return hi, (x - hi.astype(F32)).astype(BF16)


def np_halves(x):
    hi = x.astype(ml_dtypes.bfloat16)
    return hi, (x - hi.astype(np.float64)).astype(ml_dtypes.bfloat16)


@functools.cache
def tables():
    quarter = np.arange(N) + 0.25
    block = 2 * math.pi * np.outer(quarter, np.arange(N)) / N
    turn = 2 * math.pi * np.outer(quarter, np.arange(B)) / (N * B)
    lane = 2 * math.pi * (np.outer(np.arange(B), np.arange(B)) % B) / B
    hi, lo = np_halves(np.concatenate([np.cos(block), -np.sin(block)]))
    first = np.concatenate([hi, hi, lo], axis=1)
    hi, lo = np_halves(np.concatenate([np.cos(block.T), -np.sin(block.T)], axis=1) / (N * B))
    last = np.concatenate([hi, hi, lo], axis=1)
    twiddle = np.stack([np.cos(turn), np.sin(turn)]).astype(np.float32)
    c, s = np.cos(lane), np.sin(lane)
    fwd = np.stack(np_halves(np.block([[c, -s], [s, c]])))
    inv = np.stack(np_halves(np.block([[c, s], [-s, c]])))
    return first, twiddle, fwd, inv, last


def iota(shape, dim):
    return lax.broadcasted_iota(jnp.int32, shape, dim)


def wide(z, g_ref):
    hi, lo = halves(z)
    return dot(hi, g_ref[0]) + (dot(lo, g_ref[0]) + dot(hi, g_ref[1]))


def forward(src, gain, first_ref, tw_ref, fwd_ref, dst):
    cos, sin = tw_ref[0], tw_ref[1]
    first = first_ref[...]
    for c in range(C):
        x = src[pl.ds(c, N, C), :]
        if gain is not None:
            x = x * gain[:, c : c + 1]
        hi, lo = halves(x)
        y = dot(first, jnp.concatenate([hi, lo, hi], axis=0))
        re, im = y[:N], y[N:]
        dst[pl.ds(c * N, N), :] = jnp.concatenate(
            [re * cos + im * sin, im * cos - re * sin], axis=1
        )
    dst[...] = wide(dst[...], fwd_ref)


def kernel(
    *refs,
):
    given, out_ref, here = refs[:ARGS], refs[ARGS], refs[ARGS + 1 : 2 * ARGS + 1]
    scratch, load_sems = refs[2 * ARGS + 1 : -1], refs[-1]
    loads = [
        pltpu.make_async_copy(given[i], here[i], load_sems.at[i]) for i in range(ARGS)
    ]
    for load in loads:
        load.start()
    work(loads, *here, out_ref, *scratch)


def work(
    loads,
    pos_ref, rows_ref, filt_ref, w_ref, gain_ref, first_ref, tw_ref, last_ref, fwd_ref, inv_ref,
    out_ref,
    kv_send, q_send, f_send, note_send, kv_recv, q_recv, f_recv, note_recv,
    onehot, place, kv_cand, q_cand, prod, filt, spec_p, spec_f, conv, o_send, o_recv,
    send_sems, recv_sems, kv_sems, q_sems,
):
    me = lax.axis_index("ctx")
    barrier = pltpu.get_barrier_semaphore()

    def greet(k, _):
        pl.semaphore_signal(
            barrier,
            inc=1,
            device_id={"ctx": lax.rem(me + k, N)},
            device_id_type=pl.DeviceIdType.MESH,
        )
        return 0

    lax.fori_loop(1, N, greet, 0)

    loads[0].wait()
    pos = pos_ref[...]
    owner = pos // B
    across = jnp.broadcast_to(owner.astype(F32), (B, B))
    down = across.T
    earlier = (across == down) & (iota((B, B), 0) < iota((B, B), 1))
    rank = jnp.sum(jnp.where(earlier, 1.0, 0.0), axis=0, keepdims=True).astype(jnp.int32)
    code = ((owner * CAP + rank) * B + (pos - owner * B)).astype(F32)

    per = B // C

    def turned(part, j):
        return rows_ref[:, part * W + j * B : part * W + (j + 1) * B].T.reshape(per, C, B)

    loads[1].wait()
    for j in range(W // B):
        kv_send[j * per : (j + 1) * per, :C, :] = turned(1, j)
        kv_send[j * per : (j + 1) * per, C:, :] = turned(2, j)

    loads[2].wait()
    largest = jnp.maximum(jnp.max(jnp.abs(filt_ref[...]), axis=0, keepdims=True), 1e-33)
    unit = largest * (1.0 / STEPS)
    for j in range(W // B):
        note_send[j] = jnp.concatenate([code, unit[:, j * B : (j + 1) * B]], axis=0)
    mine = pl.ds(pl.multiple_of(me * C, C), C)
    note_recv[me] = note_send[me // per]

    pl.semaphore_wait(barrier, N - 1)

    def copy(src, dst, send_sem, recv_sem, to):
        return pltpu.make_async_remote_copy(
            src_ref=src,
            dst_ref=dst,
            send_sem=send_sem,
            recv_sem=recv_sem,
            device_id={"ctx": to},
            device_id_type=pl.DeviceIdType.MESH,
        )

    def send_note(k, _):
        to = lax.rem(me + k, N)
        copy(note_send.at[to // per], note_recv.at[me], send_sems.at[0], recv_sems.at[0], to).start()
        return 0

    def send_kv(k, _):
        to = lax.rem(me + k, N)
        copy(kv_send.at[to], kv_recv.at[k], send_sems.at[1], kv_sems.at[k], to).start()
        return 0

    def send_filter(k, _):
        to = lax.rem(me + k, N)
        theirs = pl.ds(pl.multiple_of(to * C, C), C)
        copy(f_send.at[theirs, :], f_recv.at[mine, :], send_sems.at[2], recv_sems.at[2], to).start()
        return 0

    def send_q(k, _):
        to = lax.rem(me + k, N)
        copy(q_send.at[to], q_recv.at[k], send_sems.at[3], q_sems.at[k], to).start()
        return 0

    lax.fori_loop(1, N, send_note, 0)
    lax.fori_loop(1, N, send_kv, 0)
    pltpu.make_async_copy(kv_send.at[me], kv_recv.at[0], kv_sems.at[0]).start()

    per_unit = STEPS / largest
    for j in range(W // B):
        part = slice(j * B, (j + 1) * B)
        steps = jnp.round(filt_ref[:, part] * per_unit[:, part]).T
        f_send[part, :] = steps.astype(jnp.int32).astype(jnp.int16)
    lax.fori_loop(1, N, send_filter, 0)
    f_recv[mine, :] = f_send[mine, :]

    for j in range(W // B):
        q_send[j * per : (j + 1) * per] = turned(0, j)
    lax.fori_loop(1, N, send_q, 0)
    pltpu.make_async_copy(q_send.at[me], q_recv.at[0], q_sems.at[0]).start()

    def arrived(part, sem):
        pltpu.make_async_copy(part, part, sem).wait()

    for load in loads[3:]:
        load.wait()

    pick = iota((C, W), 1) == me * C + iota((C, W), 0)

    def column(row):
        return jnp.sum(jnp.where(pick, row, 0.0), axis=1, keepdims=True)

    q_taps, k_taps, v_taps = (
        [column(w_ref[i : i + 1, p * W : (p + 1) * W]) for i in range(3)] for p in range(3)
    )
    kv_taps = [jnp.concatenate([k, v], axis=0) for k, v in zip(k_taps, v_taps)]
    gain = column(gain_ref[...])

    arrived(note_recv.at[pl.ds(0, N - 1)], recv_sems.at[0])

    def pair(h):
        return pl.ds(pl.multiple_of(h * 2 * CAP, 2 * CAP), 2 * CAP)

    def index(h, _):
        tiles = []
        for k in (2 * h, 2 * h + 1):
            code = note_recv[lax.rem(me - k + N, N)][:1].astype(jnp.int32)
            slot = code // B
            within = (code - slot * B + 1).astype(F32)
            hot = (iota((N * CAP, B), 0) == slot).astype(F32).astype(BF16)
            onehot[k] = hot
            at = dot(hot, jnp.broadcast_to(within, (B, B)).astype(BF16), NT)
            tile = (at == (iota((N * CAP, B), 1) + 1).astype(F32)).astype(F32)
            tiles.append(tile.reshape(N, CAP, B))
        place[:, pair(h), :] = jnp.concatenate(tiles, axis=1).astype(BF16)
        return 0

    lax.fori_loop(0, N // 2, index, 0, unroll=4)

    def spread(recv, sems, cand):
        def group(g, _):
            for i in range(8):
                k = g * 8 + i
                arrived(recv.at[k], sems.at[k])
            for i in range(4):
                h = g * 4 + i
                tiles = [
                    dot(onehot[k], recv[k], NT).reshape(N, CAP, recv.shape[1])
                    for k in (2 * h, 2 * h + 1)
                ]
                cand[:, pair(h), :] = jnp.concatenate(tiles, axis=1).astype(BF16)
            return 0

        lax.fori_loop(0, N // 8, group, 0)

    def filtered(taps, before, seq):
        lane = iota(seq.shape, 1)
        feat = taps[0] * seq
        for i in (1, 2):
            moved = jnp.where(lane < i, pltpu.roll(before, i, 1), pltpu.roll(seq, i, 1))
            feat = feat + taps[i] * moved
        return feat

    spread(kv_recv, kv_sems, kv_cand)

    def block(o, before):
        seq = dot(kv_cand[o], place[o], TN)
        feat = filtered(kv_taps, before, seq)
        prod[pl.ds(pl.multiple_of(o * C, C), C), :] = feat[:C] * feat[C:]
        return seq

    lax.fori_loop(0, N, block, jnp.zeros((2 * C, B), F32), unroll=8)

    forward(prod, None, first_ref, tw_ref, fwd_ref, spec_p)

    arrived(f_recv.at[pl.ds(0, (N - 1) * C)], recv_sems.at[2])
    filt[...] = f_recv[...].astype(jnp.int32).astype(F32)
    units = pltpu.roll(note_recv[:, 1, :], lax.rem(B - lax.rem(me, per) * C, B), 1)
    forward(filt, units, first_ref, tw_ref, fwd_ref, spec_f)

    a_re, a_im = spec_p[:, :B], spec_p[:, B:]
    b_re, b_im = spec_f[:, :B], spec_f[:, B:]
    z = jnp.concatenate([a_re * b_re - a_im * b_im, a_re * b_im + a_im * b_re], axis=1)
    spec_p[...] = wide(z, inv_ref)
    cos, sin = tw_ref[0], tw_ref[1]
    last = last_ref[...]
    for c in range(C):
        y = spec_p[pl.ds(c * N, N), :]
        re, im = y[:, :B], y[:, B:]
        hi, lo = halves(jnp.concatenate([re * cos - im * sin, im * cos + re * sin], axis=0))
        conv[pl.ds(c, N, C), :] = dot(last, jnp.concatenate([hi, lo, hi], axis=0))

    spread(q_recv, q_sems, q_cand)

    def finish(g, before):
        owners = [lax.rem(me + g * 8 + i + 1, N) for i in range(8)]
        parts = [pl.ds(pl.multiple_of(o * C, C), C) for o in owners]
        for o, theirs in zip(owners, parts):
            seq = dot(q_cand[o], place[o], TN)
            q_feat = filtered(q_taps, jnp.where(o == 0, 0.0, before), seq)
            value = q_feat * (conv[theirs, :] + gain * prod[theirs, :])
            o_send[theirs, :] = value.astype(BF16)
            before = seq

        def send(i):
            copy(o_send.at[parts[i], :], o_recv.at[mine, :], send_sems.at[4], recv_sems.at[4], owners[i]).start()

        for i in range(7):
            send(i)
        pl.when(g < N // 8 - 1)(lambda: send(7))
        return before

    lax.fori_loop(0, N // 8, finish, dot(q_cand[me], place[me], TN))
    o_recv[mine, :] = o_send[mine, :]

    most = pl.ds(0, (N - 1) * C)
    arrived(note_recv.at[pl.ds(0, N - 1)], send_sems.at[0])
    arrived(kv_send.at[pl.ds(0, N - 1)], send_sems.at[1])
    arrived(f_send.at[most], send_sems.at[2])
    arrived(q_send.at[pl.ds(0, N - 1)], send_sems.at[3])
    arrived(o_send.at[most], send_sems.at[4])
    arrived(o_recv.at[most], recv_sems.at[4])
    for j in range(W // B):
        out_ref[:, j * B : (j + 1) * B] = o_recv[j * B : (j + 1) * B, :].T


def body(loader_rows, row_pos, short_w, long_filter, skip_gain):
    first, twiddle, fwd, inv, last = (jnp.asarray(t) for t in tables())
    operands = [
        row_pos.reshape(1, B), loader_rows, long_filter, short_w, skip_gain.reshape(1, W),
        first, twiddle, last, fwd, inv,
    ]
    return pl.pallas_call(
        kernel,
        out_shape=jax.ShapeDtypeStruct((B, W), BF16),
        in_specs=[pl.BlockSpec(memory_space=pltpu.HBM)] * ARGS,
        out_specs=pl.BlockSpec(memory_space=pltpu.VMEM),
        scratch_shapes=[
            *(pltpu.VMEM(x.shape, x.dtype) for x in operands),
            pltpu.VMEM((N, 2 * C, B), BF16),
            pltpu.VMEM((N, C, B), BF16),
            pltpu.VMEM((W, B), jnp.int16),
            pltpu.VMEM((W // B, 2, B), F32),
            pltpu.VMEM((N, 2 * C, B), BF16),
            pltpu.VMEM((N, C, B), BF16),
            pltpu.VMEM((W, B), jnp.int16),
            pltpu.VMEM((N, 2, B), F32),
            pltpu.VMEM((N, N * CAP, B), BF16),
            pltpu.VMEM((N, N * CAP, B), BF16),
            pltpu.VMEM((N, N * CAP, 2 * C), BF16),
            pltpu.VMEM((N, N * CAP, C), BF16),
            pltpu.VMEM((W, B), F32),
            pltpu.VMEM((W, B), F32),
            pltpu.VMEM((W, 2 * B), F32),
            pltpu.VMEM((W, 2 * B), F32),
            pltpu.VMEM((W, B), F32),
            pltpu.VMEM((W, B), BF16),
            pltpu.VMEM((W, B), BF16),
            pltpu.SemaphoreType.DMA((5,)),
            pltpu.SemaphoreType.DMA((5,)),
            pltpu.SemaphoreType.DMA((N,)),
            pltpu.SemaphoreType.DMA((N,)),
            pltpu.SemaphoreType.DMA((ARGS,)),
        ],
        compiler_params=pltpu.CompilerParams(
            collective_id=0, has_side_effects=True, vmem_limit_bytes=60 << 20
        ),
    )(*operands)


def solution(mesh):
    return jax.shard_map(
        body,
        mesh=mesh,
        in_specs=(P("ctx", "chan"), P("ctx"), P(None, "chan"), P("ctx", "chan"), P("chan")),
        out_specs=P("ctx", "chan"),
        check_vma=False,
    )
```

time: 46.2 us -> 38.6 us (0.84)
  Pallas kernels: 44.5 us -> 36.9 us
    pallas_call x1, Pallas kernels: 44.5 us -> 36.9 us  [body(): pl.pallas_call(kernel, out_shape=jax.ShapeDtypeStruct((B, W), BF16), in_s...]
where the time goes in v3:
time: 38.6 us; the launch traced here: 38.5 us
  Pallas kernels  36.9 us (96%)
  local copies, waits for them, and re-layouts  1.57 us (4%)
    pallas_call x1, Pallas kernels, body(): pl.pallas_call(kernel, out_shape=jax.ShapeDtypeStruct((B, W), BF16), in_s...  36.9 us
    unnamed x1, local copies, waits for them, and re-layouts  1.57 us

profile of v3, /device:TPU:1, one launch (start us, length us, event | category | flops | bytes accessed | tf_op | source)
XLA Modules:
  0.0 38.5 jit_solution(13182454233054661644)
XLA Ops:
  0.0 36.9 %shard_map.100 = bf16[128,512]{1,0:T(8,128)(2,1)} custom-call(s32[1,128]{1,0:T(1,128)} %bitcast.3, bf16[128,1536]{1,0:T(8,128)(2,1)} %refs_1_.1, f32[128,512]{1,0:T(8,128)} %refs_2_.1, f32[3,1536]{1,0:T(4,128)} %refs_3_.1, f32[1,512]{1,0:T(1,128)} %bitcast.2, bf16[64,96]{1,0:T(8,128)(2,1)} %constant.10.clone.refs_5_, f32[2,32,128]{2,1,0:T(8,128)} %constant.11.clone.refs_6_, ...), custom_call_target="tpu_custom_call" | custom-call | tf_op jit(solution)/shard_map/pallas_call | solution.py:325
  36.9 1.6 %copy.12 = bf16[128,512]{1,0:T(8,128)(2,1)} copy(bf16[128,512]{1,0:T(8,128)(2,1)} %shard_map.100) | data formatting | bytes 262144

commit v4 on v3

--- a/solution.py
+++ b/solution.py
@@ -63,6 +63,11 @@
     return dot(hi, g_ref[0]) + (dot(lo, g_ref[0]) + dot(hi, g_ref[1]))
 
 
+def partner(me, step):
+    a = step // 8
+    return me ^ (jnp.where(a < 2, 2 + a, 3 - a) * 8 + 7 - step % 8)
+
+
 def forward(src, gain, first_ref, tw_ref, fwd_ref, dst):
     cos, sin = tw_ref[0], tw_ref[1]
     first = first_ref[...]
@@ -87,8 +92,6 @@
     loads = [
         pltpu.make_async_copy(given[i], here[i], load_sems.at[i]) for i in range(ARGS)
     ]
-    for load in loads:
-        load.start()
     work(loads, *here, out_ref, *scratch)
 
 
@@ -97,22 +100,24 @@
     pos_ref, rows_ref, filt_ref, w_ref, gain_ref, first_ref, tw_ref, last_ref, fwd_ref, inv_ref,
     out_ref,
     kv_send, q_send, f_send, note_send, kv_recv, q_recv, f_recv, note_recv,
-    onehot, place, kv_cand, q_cand, prod, filt, spec_p, spec_f, conv, o_send, o_recv,
+    onehot, place, kv_cand, q_cand, q_feat, prod, filt, spec_p, spec_f, conv, o_send, o_recv,
     send_sems, recv_sems, kv_sems, q_sems,
 ):
     me = lax.axis_index("ctx")
     barrier = pltpu.get_barrier_semaphore()
 
-    def greet(k, _):
+    def greet(step, _):
         pl.semaphore_signal(
             barrier,
             inc=1,
-            device_id={"ctx": lax.rem(me + k, N)},
+            device_id={"ctx": partner(me, step)},
             device_id_type=pl.DeviceIdType.MESH,
         )
         return 0
 
-    lax.fori_loop(1, N, greet, 0)
+    lax.fori_loop(0, N - 1, greet, 0)
+    for load in loads:
+        load.start()
 
     loads[0].wait()
     pos = pos_ref[...]
@@ -153,43 +158,50 @@
             device_id_type=pl.DeviceIdType.MESH,
         )
 
-    def send_note(k, _):
-        to = lax.rem(me + k, N)
+    def send_note(step, _):
+        to = partner(me, step)
         copy(note_send.at[to // per], note_recv.at[me], send_sems.at[0], recv_sems.at[0], to).start()
         return 0
 
-    def send_kv(k, _):
-        to = lax.rem(me + k, N)
-        copy(kv_send.at[to], kv_recv.at[k], send_sems.at[1], kv_sems.at[k], to).start()
-        return 0
-
-    def send_filter(k, _):
-        to = lax.rem(me + k, N)
-        theirs = pl.ds(pl.multiple_of(to * C, C), C)
-        copy(f_send.at[theirs, :], f_recv.at[mine, :], send_sems.at[2], recv_sems.at[2], to).start()
-        return 0
-
-    def send_q(k, _):
-        to = lax.rem(me + k, N)
-        copy(q_send.at[to], q_recv.at[k], send_sems.at[3], q_sems.at[k], to).start()
-        return 0
-
-    lax.fori_loop(1, N, send_note, 0)
-    lax.fori_loop(1, N, send_kv, 0)
-    pltpu.make_async_copy(kv_send.at[me], kv_recv.at[0], kv_sems.at[0]).start()
+    def send_kv(step, _):
+        to = partner(me, step)
+        copy(kv_send.at[to], kv_recv.at[step], send_sems.at[1], kv_sems.at[step], to).start()
+        return 0
+
+    def send_q(step, _):
+        to = partner(me, step)
+        copy(q_send.at[to], q_recv.at[step], send_sems.at[3], q_sems.at[step], to).start()
+        return 0
+
+    def channels_of(to):
+        return pl.ds(pl.multiple_of(to * C, C), C)
+
+    def send_filter(step, _):
+        to = partner(me, step)
+        copy(f_send.at[channels_of(to), :], f_recv.at[mine, :], send_sems.at[2], recv_sems.at[2], to).start()
+        return 0
+
+    def send_out(step, _):
+        to = partner(me, step)
+        copy(o_send.at[channels_of(to), :], o_recv.at[mine, :], send_sems.at[4], recv_sems.at[4], to).start()
+        return 0
+
+    lax.fori_loop(0, N - 1, send_note, 0)
+    lax.fori_loop(0, N - 1, send_kv, 0)
+    pltpu.make_async_copy(kv_send.at[me], kv_recv.at[N - 1], kv_sems.at[N - 1]).start()
+
+    for j in range(W // B):
+        q_send[j * per : (j + 1) * per] = turned(0, j)
+    lax.fori_loop(0, N - 1, send_q, 0)
+    pltpu.make_async_copy(q_send.at[me], q_recv.at[N - 1], q_sems.at[N - 1]).start()
 
     per_unit = STEPS / largest
     for j in range(W // B):
         part = slice(j * B, (j + 1) * B)
         steps = jnp.round(filt_ref[:, part] * per_unit[:, part]).T
         f_send[part, :] = steps.astype(jnp.int32).astype(jnp.int16)
-    lax.fori_loop(1, N, send_filter, 0)
+    lax.fori_loop(0, N - 1, send_filter, 0)
     f_recv[mine, :] = f_send[mine, :]
-
-    for j in range(W // B):
-        q_send[j * per : (j + 1) * per] = turned(0, j)
-    lax.fori_loop(1, N, send_q, 0)
-    pltpu.make_async_copy(q_send.at[me], q_recv.at[0], q_sems.at[0]).start()
 
     def arrived(part, sem):
         pltpu.make_async_copy(part, part, sem).wait()
@@ -216,7 +228,7 @@
     def index(h, _):
         tiles = []
         for k in (2 * h, 2 * h + 1):
-            code = note_recv[lax.rem(me - k + N, N)][:1].astype(jnp.int32)
+            code = note_recv[partner(me, k)][:1].astype(jnp.int32)
             slot = code // B
             within = (code - slot * B + 1).astype(F32)
             hot = (iota((N * CAP, B), 0) == slot).astype(F32).astype(BF16)
@@ -265,6 +277,15 @@
 
     forward(prod, None, first_ref, tw_ref, fwd_ref, spec_p)
 
+    spread(q_recv, q_sems, q_cand)
+
+    def q_block(o, before):
+        seq = dot(q_cand[o], place[o], TN)
+        q_feat[pl.ds(pl.multiple_of(o * C, C), C), :] = filtered(q_taps, before, seq)
+        return seq
+
+    lax.fori_loop(0, N, q_block, jnp.zeros((C, B), F32), unroll=8)
+
     arrived(f_recv.at[pl.ds(0, (N - 1) * C)], recv_sems.at[2])
     filt[...] = f_recv[...].astype(jnp.int32).astype(F32)
     units = pltpu.roll(note_recv[:, 1, :], lax.rem(B - lax.rem(me, per) * C, B), 1)
@@ -282,38 +303,23 @@
         hi, lo = halves(jnp.concatenate([re * cos - im * sin, im * cos + re * sin], axis=0))
         conv[pl.ds(c, N, C), :] = dot(last, jnp.concatenate([hi, lo, hi], axis=0))
 
-    spread(q_recv, q_sems, q_cand)
-
-    def finish(g, before):
-        owners = [lax.rem(me + g * 8 + i + 1, N) for i in range(8)]
-        parts = [pl.ds(pl.multiple_of(o * C, C), C) for o in owners]
-        for o, theirs in zip(owners, parts):
-            seq = dot(q_cand[o], place[o], TN)
-            q_feat = filtered(q_taps, jnp.where(o == 0, 0.0, before), seq)
-            value = q_feat * (conv[theirs, :] + gain * prod[theirs, :])
-            o_send[theirs, :] = value.astype(BF16)
-            before = seq
-
-        def send(i):
-            copy(o_send.at[parts[i], :], o_recv.at[mine, :], send_sems.at[4], recv_sems.at[4], owners[i]).start()
-
-        for i in range(7):
-            send(i)
-        pl.when(g < N // 8 - 1)(lambda: send(7))
-        return before
-
-    lax.fori_loop(0, N // 8, finish, dot(q_cand[me], place[me], TN))
+    def blocks(ref):
+        return ref[...].reshape(N, C, B)
+
+    gated = blocks(q_feat) * (blocks(conv) + gain[None] * blocks(prod))
+    o_send[...] = gated.astype(BF16).reshape(W, B)
+    lax.fori_loop(0, N - 1, send_out, 0)
     o_recv[mine, :] = o_send[mine, :]
 
     most = pl.ds(0, (N - 1) * C)
+    arrived(o_recv.at[most], recv_sems.at[4])
+    for j in range(W // B):
+        out_ref[:, j * B : (j + 1) * B] = o_recv[j * B : (j + 1) * B, :].T
     arrived(note_recv.at[pl.ds(0, N - 1)], send_sems.at[0])
     arrived(kv_send.at[pl.ds(0, N - 1)], send_sems.at[1])
     arrived(f_send.at[most], send_sems.at[2])
     arrived(q_send.at[pl.ds(0, N - 1)], send_sems.at[3])
     arrived(o_send.at[most], send_sems.at[4])
-    arrived(o_recv.at[most], recv_sems.at[4])
-    for j in range(W // B):
-        out_ref[:, j * B : (j + 1) * B] = o_recv[j * B : (j + 1) * B, :].T
 
 
 def body(loader_rows, row_pos, short_w, long_filter, skip_gain):
@@ -324,7 +330,7 @@
     ]
     return pl.pallas_call(
         kernel,
-        out_shape=jax.ShapeDtypeStruct((B, W), BF16),
+        out_shape=pltpu.VMEM((B, W), BF16),
         in_specs=[pl.BlockSpec(memory_space=pltpu.HBM)] * ARGS,
         out_specs=pl.BlockSpec(memory_space=pltpu.VMEM),
         scratch_shapes=[
@@ -343,6 +349,7 @@
             pltpu.VMEM((N, N * CAP, C), BF16),
             pltpu.VMEM((W, B), F32),
             pltpu.VMEM((W, B), F32),
+            pltpu.VMEM((W, B), F32),
             pltpu.VMEM((W, 2 * B), F32),
             pltpu.VMEM((W, 2 * B), F32),
             pltpu.VMEM((W, B), F32),
@@ -355,7 +362,7 @@
             pltpu.SemaphoreType.DMA((ARGS,)),
         ],
         compiler_params=pltpu.CompilerParams(
-            collective_id=0, has_side_effects=True, vmem_limit_bytes=60 << 20
+            collective_id=0, has_side_effects=True, vmem_limit_bytes=54 << 20
         ),
     )(*operands)
 

time: 38.6 us -> 35.7 us (0.925)
  Pallas kernels: 36.9 us -> 34.9 us
  local copies, waits for them, and re-layouts: 1.57 us -> 0.66 us
    pallas_call x1, Pallas kernels: 36.9 us -> 34.9 us  [body(): pl.pallas_call(kernel, out_shape=pltpu.VMEM((B, W), BF16), in_specs=[pl.B...]
    unnamed x1, local copies, waits for them, and re-layouts: 1.57 us -> 0.66 us
where the time goes in v4:
time: 35.7 us; the launch traced here: 35.6 us
  Pallas kernels  34.9 us (98%)
  local copies, waits for them, and re-layouts  0.66 us (2%)
    pallas_call x1, Pallas kernels, body(): pl.pallas_call(kernel, out_shape=pltpu.VMEM((B, W), BF16), in_specs=[pl.B...  34.9 us

profile of v4, /device:TPU:1, one launch (start us, length us, event | category | flops | bytes accessed | tf_op | source)
XLA Modules:
  0.0 35.6 jit_solution(107027058892483691)
XLA Ops:
  0.0 34.9 %shard_map.100 = bf16[128,512]{1,0:T(8,128)(2,1)S(1)} custom-call(s32[1,128]{1,0:T(1,128)} %bitcast.3, bf16[128,1536]{1,0:T(8,128)(2,1)} %refs_1_.1, f32[128,512]{1,0:T(8,128)} %refs_2_.1, f32[3,1536]{1,0:T(4,128)} %refs_3_.1, f32[1,512]{1,0:T(1,128)} %bitcast.2, bf16[64,96]{1,0:T(8,128)(2,1)} %constant.10.clone.refs_5_, ...), custom_call_target="tpu_custom_call" | custom-call | tf_op jit(solution)/shard_map/pallas_call | solution.py:331
  35.0 0.7 %copy.12 = bf16[128,512]{1,0:T(8,128)(2,1)} copy(bf16[128,512]{1,0:T(8,128)(2,1)S(1)} %shard_map.100) | data formatting | bytes 262144

commit v5 on v4

--- a/solution.py
+++ b/solution.py
@@ -15,6 +15,7 @@
 C = 16
 W = 512
 ARGS = 10
+LEVEL = 32768.0
 STEPS = 32767.0
 CAP = 8
 F32, BF16 = jnp.float32, jnp.bfloat16
@@ -25,6 +26,10 @@
 
 def dot(a, b, dims=NN):
     return lax.dot_general(a, b, dims, preferred_element_type=F32)
+
+
+def unit_of(level):
+    return jnp.exp2((level - 256.0) * 0.5)
 
 
 def halves(x):
@@ -140,9 +145,10 @@
 
     loads[2].wait()
     largest = jnp.maximum(jnp.max(jnp.abs(filt_ref[...]), axis=0, keepdims=True), 1e-33)
-    unit = largest * (1.0 / STEPS)
-    for j in range(W // B):
-        note_send[j] = jnp.concatenate([code, unit[:, j * B : (j + 1) * B]], axis=0)
+    level = jnp.clip(jnp.ceil(2.0 * jnp.log2(largest * (1.0 / STEPS))) + 256.0, 1.0, 254.0)
+    level = jnp.where(unit_of(level) * STEPS < largest, level + 1.0, level)
+    for j in range(W // B):
+        note_send[j] = level[:, j * B : (j + 1) * B] * LEVEL + code
     mine = pl.ds(pl.multiple_of(me * C, C), C)
     note_recv[me] = note_send[me // per]
 
@@ -195,7 +201,7 @@
     lax.fori_loop(0, N - 1, send_q, 0)
     pltpu.make_async_copy(q_send.at[me], q_recv.at[N - 1], q_sems.at[N - 1]).start()
 
-    per_unit = STEPS / largest
+    per_unit = 1.0 / unit_of(level)
     for j in range(W // B):
         part = slice(j * B, (j + 1) * B)
         steps = jnp.round(filt_ref[:, part] * per_unit[:, part]).T
@@ -228,7 +234,8 @@
     def index(h, _):
         tiles = []
         for k in (2 * h, 2 * h + 1):
-            code = note_recv[partner(me, k)][:1].astype(jnp.int32)
+            note = note_recv[partner(me, k)]
+            code = (note - jnp.floor(note * (1.0 / LEVEL)) * LEVEL).astype(jnp.int32)
             slot = code // B
             within = (code - slot * B + 1).astype(F32)
             hot = (iota((N * CAP, B), 0) == slot).astype(F32).astype(BF16)
@@ -288,7 +295,8 @@
 
     arrived(f_recv.at[pl.ds(0, (N - 1) * C)], recv_sems.at[2])
     filt[...] = f_recv[...].astype(jnp.int32).astype(F32)
-    units = pltpu.roll(note_recv[:, 1, :], lax.rem(B - lax.rem(me, per) * C, B), 1)
+    units = unit_of(jnp.floor(note_recv[:, 0, :] * (1.0 / LEVEL)))
+    units = pltpu.roll(units, lax.rem(B - lax.rem(me, per) * C, B), 1)
     forward(filt, units, first_ref, tw_ref, fwd_ref, spec_f)
 
     a_re, a_im = spec_p[:, :B], spec_p[:, B:]
@@ -338,11 +346,11 @@
             pltpu.VMEM((N, 2 * C, B), BF16),
             pltpu.VMEM((N, C, B), BF16),
             pltpu.VMEM((W, B), jnp.int16),
-            pltpu.VMEM((W // B, 2, B), F32),
+            pltpu.VMEM((W // B, 1, B), F32),
             pltpu.VMEM((N, 2 * C, B), BF16),
             pltpu.VMEM((N, C, B), BF16),
             pltpu.VMEM((W, B), jnp.int16),
-            pltpu.VMEM((N, 2, B), F32),
+            pltpu.VMEM((N, 1, B), F32),
             pltpu.VMEM((N, N * CAP, B), BF16),
             pltpu.VMEM((N, N * CAP, B), BF16),
             pltpu.VMEM((N, N * CAP, 2 * C), BF16),

time: 35.7 us -> 35 us (0.980)
  Pallas kernels: 34.9 us -> 34.2 us
    pallas_call x1, Pallas kernels: 34.9 us -> 34.2 us  [body(): pl.pallas_call(kernel, out_shape=pltpu.VMEM((B, W), BF16), in_specs=[pl.B...]
where the time goes in v5:
time: 35 us; the launch traced here: 34.9 us
  Pallas kernels  34.2 us (98%)
  local copies, waits for them, and re-layouts  0.66 us (2%)
    pallas_call x1, Pallas kernels, body(): pl.pallas_call(kernel, out_shape=pltpu.VMEM((B, W), BF16), in_specs=[pl.B...  34.2 us

profile of v5, /device:TPU:1, one launch (start us, length us, event | category | flops | bytes accessed | tf_op | source)
XLA Modules:
  0.0 34.9 jit_solution(15821121487031695844)
XLA Ops:
  0.0 34.2 %shard_map.100 = bf16[128,512]{1,0:T(8,128)(2,1)S(1)} custom-call(s32[1,128]{1,0:T(1,128)} %bitcast.3, bf16[128,1536]{1,0:T(8,128)(2,1)} %refs_1_.1, f32[128,512]{1,0:T(8,128)} %refs_2_.1, f32[3,1536]{1,0:T(4,128)} %refs_3_.1, f32[1,512]{1,0:T(1,128)} %bitcast.2, bf16[64,96]{1,0:T(8,128)(2,1)} %constant.10.clone.refs_5_, ...), custom_call_target="tpu_custom_call" | custom-call | tf_op jit(solution)/shard_map/pallas_call | solution.py:339
  34.2 0.7 %copy.12 = bf16[128,512]{1,0:T(8,128)(2,1)} copy(bf16[128,512]{1,0:T(8,128)(2,1)S(1)} %shard_map.100) | data formatting | bytes 262144

commit v6 on v5

--- a/solution.py
+++ b/solution.py
@@ -29,7 +29,7 @@
 
 
 def unit_of(level):
-    return jnp.exp2((level - 256.0) * 0.5)
+    return jnp.exp2((level - 512.0) * 0.25)
 
 
 def halves(x):
@@ -54,8 +54,10 @@
     last = np.concatenate([hi, hi, lo], axis=1)
     twiddle = np.stack([np.cos(turn), np.sin(turn)]).astype(np.float32)
     c, s = np.cos(lane), np.sin(lane)
-    fwd = np.stack(np_halves(np.block([[c, -s], [s, c]])))
-    inv = np.stack(np_halves(np.block([[c, s], [-s, c]])))
+    hi, lo = np_halves(np.block([[c, -s], [s, c]]))
+    fwd = np.concatenate([hi, hi, lo])
+    hi, lo = np_halves(np.block([[c, s], [-s, c]]))
+    inv = np.concatenate([hi, hi, lo])
     return first, twiddle, fwd, inv, last
 
 
@@ -65,7 +67,7 @@
 
 def wide(z, g_ref):
     hi, lo = halves(z)
-    return dot(hi, g_ref[0]) + (dot(lo, g_ref[0]) + dot(hi, g_ref[1]))
+    return dot(jnp.concatenate([hi, lo, hi], axis=1), g_ref[...])
 
 
 def partner(me, step):
@@ -76,16 +78,18 @@
 def forward(src, gain, first_ref, tw_ref, fwd_ref, dst):
     cos, sin = tw_ref[0], tw_ref[1]
     first = first_ref[...]
-    for c in range(C):
-        x = src[pl.ds(c, N, C), :]
+    for start in range(0, C, 2):
+        group = range(start, start + 2)
+        parts = [src[pl.ds(c, N, C), :] for c in group]
         if gain is not None:
-            x = x * gain[:, c : c + 1]
-        hi, lo = halves(x)
+            parts = [x * gain[:, c : c + 1] for c, x in zip(group, parts)]
+        hi, lo = halves(jnp.concatenate(parts, axis=1))
         y = dot(first, jnp.concatenate([hi, lo, hi], axis=0))
-        re, im = y[:N], y[N:]
-        dst[pl.ds(c * N, N), :] = jnp.concatenate(
-            [re * cos + im * sin, im * cos - re * sin], axis=1
-        )
+        for i, c in enumerate(group):
+            re, im = y[:N, i * B : (i + 1) * B], y[N:, i * B : (i + 1) * B]
+            dst[pl.ds(c * N, N), :] = jnp.concatenate(
+                [re * cos + im * sin, im * cos - re * sin], axis=1
+            )
     dst[...] = wide(dst[...], fwd_ref)
 
 
@@ -145,7 +149,7 @@
 
     loads[2].wait()
     largest = jnp.maximum(jnp.max(jnp.abs(filt_ref[...]), axis=0, keepdims=True), 1e-33)
-    level = jnp.clip(jnp.ceil(2.0 * jnp.log2(largest * (1.0 / STEPS))) + 256.0, 1.0, 254.0)
+    level = jnp.clip(jnp.ceil(4.0 * jnp.log2(largest * (1.0 / STEPS))) + 512.0, 1.0, 510.0)
     level = jnp.where(unit_of(level) * STEPS < largest, level + 1.0, level)
     for j in range(W // B):
         note_send[j] = level[:, j * B : (j + 1) * B] * LEVEL + code
@@ -305,11 +309,17 @@
     spec_p[...] = wide(z, inv_ref)
     cos, sin = tw_ref[0], tw_ref[1]
     last = last_ref[...]
-    for c in range(C):
-        y = spec_p[pl.ds(c * N, N), :]
-        re, im = y[:, :B], y[:, B:]
-        hi, lo = halves(jnp.concatenate([re * cos - im * sin, im * cos + re * sin], axis=0))
-        conv[pl.ds(c, N, C), :] = dot(last, jnp.concatenate([hi, lo, hi], axis=0))
+    for start in range(0, C, 2):
+        group = range(start, start + 2)
+        parts = []
+        for c in group:
+            y = spec_p[pl.ds(c * N, N), :]
+            re, im = y[:, :B], y[:, B:]
+            parts.append(jnp.concatenate([re * cos - im * sin, im * cos + re * sin], axis=0))
+        hi, lo = halves(jnp.concatenate(parts, axis=1))
+        y = dot(last, jnp.concatenate([hi, lo, hi], axis=0))
+        for i, c in enumerate(group):
+            conv[pl.ds(c, N, C), :] = y[:, i * B : (i + 1) * B]
 
     def blocks(ref):
         return ref[...].reshape(N, C, B)

time: 35 us -> 34.9 us (level)
  no operation moved by 1% of the time
where the time goes in v6:
time: 34.9 us; the launch traced here: 34.8 us
  Pallas kernels  34.2 us (98%)
  local copies, waits for them, and re-layouts  0.66 us (2%)
    pallas_call x1, Pallas kernels, body(): pl.pallas_call(kernel, out_shape=pltpu.VMEM((B, W), BF16), in_specs=[pl.B...  34.2 us

profile of v6, /device:TPU:1, one launch (start us, length us, event | category | flops | bytes accessed | tf_op | source)
XLA Modules:
  0.0 34.8 jit_solution(6734571981530395170)
XLA Ops:
  0.0 34.2 %shard_map.100 = bf16[128,512]{1,0:T(8,128)(2,1)S(1)} custom-call(s32[1,128]{1,0:T(1,128)} %bitcast.3, bf16[128,1536]{1,0:T(8,128)(2,1)} %refs_1_.1, f32[128,512]{1,0:T(8,128)} %refs_2_.1, f32[3,1536]{1,0:T(4,128)} %refs_3_.1, f32[1,512]{1,0:T(1,128)} %bitcast.2, bf16[64,96]{1,0:T(8,128)(2,1)} %constant.10.clone.refs_5_, ...), custom_call_target="tpu_custom_call" | custom-call | tf_op jit(solution)/shard_map/pallas_call | solution.py:349
  34.2 0.7 %copy.12 = bf16[128,512]{1,0:T(8,128)(2,1)} copy(bf16[128,512]{1,0:T(8,128)(2,1)S(1)} %shard_map.100) | data formatting | bytes 262144

commit v7 on v6

--- a/solution.py
+++ b/solution.py
@@ -321,18 +321,21 @@
         for i, c in enumerate(group):
             conv[pl.ds(c, N, C), :] = y[:, i * B : (i + 1) * B]
 
-    def blocks(ref):
-        return ref[...].reshape(N, C, B)
-
-    gated = blocks(q_feat) * (blocks(conv) + gain[None] * blocks(prod))
-    o_send[...] = gated.astype(BF16).reshape(W, B)
-    lax.fori_loop(0, N - 1, send_out, 0)
+    for start in range(0, N, 8):
+        first_owner = partner(me, start) // 8 * 8
+        plane = pl.ds(pl.multiple_of(first_owner * C, 8 * C), 8 * C)
+
+        def blocks(ref):
+            return ref[plane, :].reshape(8, C, B)
+
+        gated = blocks(q_feat) * (blocks(conv) + gain[None] * blocks(prod))
+        o_send[plane, :] = gated.astype(BF16).reshape(8 * C, B)
+        lax.fori_loop(start, min(start + 8, N - 1), send_out, 0)
     o_recv[mine, :] = o_send[mine, :]
 
     most = pl.ds(0, (N - 1) * C)
     arrived(o_recv.at[most], recv_sems.at[4])
-    for j in range(W // B):
-        out_ref[:, j * B : (j + 1) * B] = o_recv[j * B : (j + 1) * B, :].T
+    out_ref[...] = o_recv[...]
     arrived(note_recv.at[pl.ds(0, N - 1)], send_sems.at[0])
     arrived(kv_send.at[pl.ds(0, N - 1)], send_sems.at[1])
     arrived(f_send.at[most], send_sems.at[2])
@@ -346,9 +349,9 @@
         row_pos.reshape(1, B), loader_rows, long_filter, short_w, skip_gain.reshape(1, W),
         first, twiddle, last, fwd, inv,
     ]
-    return pl.pallas_call(
+    turned = pl.pallas_call(
         kernel,
-        out_shape=pltpu.VMEM((B, W), BF16),
+        out_shape=pltpu.VMEM((W, B), BF16),
         in_specs=[pl.BlockSpec(memory_space=pltpu.HBM)] * ARGS,
         out_specs=pl.BlockSpec(memory_space=pltpu.VMEM),
         scratch_shapes=[
@@ -383,6 +386,7 @@
             collective_id=0, has_side_effects=True, vmem_limit_bytes=54 << 20
         ),
     )(*operands)
+    return turned.T
 
 
 def solution(mesh):

time: 34.9 us -> 34.9 us (level)
    transpose x0 -> x1, local copies, waits for them, and re-layouts: none -> 0.77 us  [body(): return turned.T]
    unnamed x1 -> x0, local copies, waits for them, and re-layouts: 0.66 us -> none
where the time goes in v7:
time: 34.9 us
  Pallas kernels  34.1 us (98%)
  local copies, waits for them, and re-layouts  0.77 us (2%)
    pallas_call x1, Pallas kernels, body(): pl.pallas_call(kernel, out_shape=pltpu.VMEM((W, B), BF16), in_specs=[pl.B...  34.1 us
    transpose x1, local copies, waits for them, and re-layouts, body(): return turned.T  0.77 us

profile of v7, /device:TPU:1, one launch (start us, length us, event | category | flops | bytes accessed | tf_op | source)
XLA Modules:
  0.0 34.9 jit_solution(7719449126125758816)
XLA Ops:
  0.0 34.1 %shard_map.100 = bf16[512,128]{1,0:T(8,128)(2,1)S(1)} custom-call(s32[1,128]{1,0:T(1,128)} %bitcast.5, bf16[128,1536]{1,0:T(8,128)(2,1)} %refs_1_.1, f32[128,512]{1,0:T(8,128)} %refs_2_.1, f32[3,1536]{1,0:T(4,128)} %refs_3_.1, f32[1,512]{1,0:T(1,128)} %bitcast.4, bf16[64,96]{1,0:T(8,128)(2,1)} %constant.10.clone.refs_5_, ...), custom_call_target="tpu_custom_call" | custom-call | tf_op jit(solution)/shard_map/pallas_call | solution.py:352
  34.1 0.8 %copy.11 = bf16[128,512]{1,0:T(8,128)(2,1)} copy(bf16[128,512]{0,1:T(8,128)(2,1)S(1)} %bitcast.3) | data formatting | bytes 262144 | tf_op jit(solution)/shard_map/transpose | solution.py:389

commit v8 on v7

--- a/solution.py
+++ b/solution.py
@@ -109,7 +109,7 @@
     pos_ref, rows_ref, filt_ref, w_ref, gain_ref, first_ref, tw_ref, last_ref, fwd_ref, inv_ref,
     out_ref,
     kv_send, q_send, f_send, note_send, kv_recv, q_recv, f_recv, note_recv,
-    onehot, place, kv_cand, q_cand, q_feat, prod, filt, spec_p, spec_f, conv, o_send, o_recv,
+    onehot, place, kv_cand, q_cand, q_feat, prod, filt, spec_p, spec_f, conv, o_send,
     send_sems, recv_sems, kv_sems, q_sems,
 ):
     me = lax.axis_index("ctx")
@@ -193,7 +193,7 @@
 
     def send_out(step, _):
         to = partner(me, step)
-        copy(o_send.at[channels_of(to), :], o_recv.at[mine, :], send_sems.at[4], recv_sems.at[4], to).start()
+        copy(o_send.at[channels_of(to), :], out_ref.at[mine, :], send_sems.at[4], recv_sems.at[4], to).start()
         return 0
 
     lax.fori_loop(0, N - 1, send_note, 0)
@@ -331,11 +331,10 @@
         gated = blocks(q_feat) * (blocks(conv) + gain[None] * blocks(prod))
         o_send[plane, :] = gated.astype(BF16).reshape(8 * C, B)
         lax.fori_loop(start, min(start + 8, N - 1), send_out, 0)
-    o_recv[mine, :] = o_send[mine, :]
+    out_ref[mine, :] = o_send[mine, :]
 
     most = pl.ds(0, (N - 1) * C)
-    arrived(o_recv.at[most], recv_sems.at[4])
-    out_ref[...] = o_recv[...]
+    arrived(out_ref.at[most], recv_sems.at[4])
     arrived(note_recv.at[pl.ds(0, N - 1)], send_sems.at[0])
     arrived(kv_send.at[pl.ds(0, N - 1)], send_sems.at[1])
     arrived(f_send.at[most], send_sems.at[2])
@@ -375,7 +374,6 @@
             pltpu.VMEM((W, 2 * B), F32),
             pltpu.VMEM((W, B), F32),
             pltpu.VMEM((W, B), BF16),
-            pltpu.VMEM((W, B), BF16),
             pltpu.SemaphoreType.DMA((5,)),
             pltpu.SemaphoreType.DMA((5,)),
             pltpu.SemaphoreType.DMA((N,)),

time: 34.9 us -> 34.9 us (level)
  no operation moved by 1% of the time
where the time goes in v8:
time: 34.9 us; the launch traced here: 34.8 us
  Pallas kernels  34.1 us (98%)
  local copies, waits for them, and re-layouts  0.77 us (2%)
    pallas_call x1, Pallas kernels, body(): pl.pallas_call(kernel, out_shape=pltpu.VMEM((W, B), BF16), in_specs=[pl.B...  34.1 us
    transpose x1, local copies, waits for them, and re-layouts, body(): return turned.T  0.77 us

profile of v8, /device:TPU:1, one launch (start us, length us, event | category | flops | bytes accessed | tf_op | source)
XLA Modules:
  0.0 34.8 jit_solution(7379902787343855902)
XLA Ops:
  0.0 34.1 %shard_map.100 = bf16[512,128]{1,0:T(8,128)(2,1)S(1)} custom-call(s32[1,128]{1,0:T(1,128)} %bitcast.5, bf16[128,1536]{1,0:T(8,128)(2,1)} %refs_1_.1, f32[128,512]{1,0:T(8,128)} %refs_2_.1, f32[3,1536]{1,0:T(4,128)} %refs_3_.1, f32[1,512]{1,0:T(1,128)} %bitcast.4, bf16[64,96]{1,0:T(8,128)(2,1)} %constant.10.clone.refs_5_, ...), custom_call_target="tpu_custom_call" | custom-call | tf_op jit(solution)/shard_map/pallas_call | solution.py:351
  34.1 0.8 %copy.11 = bf16[128,512]{1,0:T(8,128)(2,1)} copy(bf16[128,512]{0,1:T(8,128)(2,1)S(1)} %bitcast.3) | data formatting | bytes 262144 | tf_op jit(solution)/shard_map/transpose | solution.py:387
